TPU v7x, 256 devices: a whole 4x4x8 slice. The times are simulated.
256 devices in a mesh: grp: 16 (over z, y_lo), ep: 16 (over y_hi, x, core).
Axes of the slice: x: 4, y: 4 (y_hi: 2, y_lo: 2; y = y_hi * 2 + y_lo), z: 8, core: 2. Of those that a mesh axis runs over, the one named last changes fastest.
Arguments:
- expert_ids: int32 [2, 16384, 6], P(None, ('grp', 'ep')), may hold values from 0 to 15, all different within a row; in each aligned block of 64 rows (0 to 63, 64 to 127, ..., all dimensions but the last counted through in order) at most 32 rows name the same one
- gates: float32 [2, 16384, 6], P(None, ('grp', 'ep')), may hold values from 0.1 to 1
- hidden: bfloat16 [2, 16384, 6, 768], P(None, ('grp', 'ep')), may hold values from -4 to 4
- cotangent: bfloat16 [2, 16384, 2560], P(None, ('grp', 'ep')), may hold values from -6 to 6
- old_place: int32 [16], replicated, may hold values from 0 to 15, as said below
- new_place: int32 [16], replicated, may hold values from 0 to 15, as said below
- old_weights: bfloat16 [16, 768, 2560], P('ep'), may hold values from -0.21875 to 0.21875
Outputs:
- slot_grads: bfloat16 [2, 16384, 6, 768], P(None, ('grp', 'ep'))
- new_weights: bfloat16 [16, 768, 2560], P('ep')
- expert_grads: bfloat16 [16, 768, 2560], P('ep', None, 'grp')
Inputs may be any that keep to these rules, and one draw needn't show every extreme that they name: `expert_ids`: each row names 6 different experts; within one micro-batch no expert is named by more than 32 of the 64 tokens of one device, and some expert reaches 32. A permutation of the slots: expert e sits in slot old_place[e]. A permutation of the slots: expert e sits in slot new_place[e].
All inputs are finite; a program needn't handle non-finite values.
Results may differ from a plain program's by a relative error of at most 0.024.
Values may be sent and summed in bfloat16 or wider, within the bound.
A program may use at most 128 MiB of HBM per device.

v0:
```python
import jax
import jax.numpy as jnp
from jax import lax
from jax.sharding import PartitionSpec as P


def local(expert_ids, gates, hidden, cotangent, old_place, new_place, old_weights):
    ep_count = lax.axis_size("ep")
    grp_count = lax.axis_size("grp")
    slots_here, width_h, width_d = old_weights.shape
    experts = old_place.shape[0]
    micro_count, tok_rows, top_count = expert_ids.shape
    capacity = min(tok_rows, 4 * tok_rows * top_count // (3 * experts))
    ep_rank = lax.axis_index("ep")
    grp_rank = lax.axis_index("grp")
    share_width = width_d // grp_count
    numbers = jnp.arange(experts, dtype=jnp.int32)
    match_old = old_place[:, None] == numbers[None, :]
    moved_slot = jnp.sum(jnp.where(match_old, new_place[:, None], 0), axis=0)
    match_new = new_place[:, None] == numbers[None, :]
    anchor_slot = jnp.sum(jnp.where(match_new, old_place[:, None], 0), axis=0)
    targets = lax.dynamic_slice_in_dim(moved_slot, ep_rank * slots_here, slots_here) // slots_here
    sources = lax.dynamic_slice_in_dim(anchor_slot, ep_rank * slots_here, slots_here)
    peer_ids = jnp.arange(ep_count, dtype=jnp.int32)
    route_mask = peer_ids[:, None] == targets[None, :]

    def outbound(share):
        spread = jnp.broadcast_to(share[None], (ep_count,) + share.shape)
        return jnp.where(route_mask[:, :, None, None], spread, jnp.zeros_like(spread))

    def inbound(received):
        flat_recv = received.reshape((ep_count * slots_here,) + received.shape[2:])
        return jnp.take(flat_recv, sources, axis=0)

    weight_share = lax.dynamic_slice_in_dim(old_weights, grp_rank * share_width, share_width, 2)
    moved_rows = lax.all_to_all(
        outbound(weight_share), "ep", split_axis=0, concat_axis=0, tiled=True
    )
    new_weights = lax.all_gather(inbound(moved_rows), "grp", axis=2, tiled=True)

    def expert_pass(routed, gate_rows, hid_rows, cot_rows, place, weights):
        flat_ids = routed.reshape(-1)
        onehot = (flat_ids[:, None] == numbers[None, :]).astype(jnp.int32)
        before = jnp.cumsum(onehot, axis=0) - onehot
        position = jnp.sum(before * onehot, axis=1)
        slot_ids = jnp.sum(onehot * place[None, :], axis=1)
        buffer_rows = slot_ids * capacity + position
        scaled = (gate_rows[:, :, None] * cot_rows[:, None, :].astype(jnp.float32)).astype(
            jnp.bfloat16
        )
        scaled = scaled.reshape(-1, width_d)
        total_rows = experts * capacity
        scaled_buf = jnp.zeros((total_rows, width_d), jnp.bfloat16).at[buffer_rows].set(scaled)
        scaled_buf = scaled_buf.reshape(ep_count, slots_here, capacity, width_d)
        hid_buf = (
            jnp.zeros((total_rows, width_h), jnp.bfloat16)
            .at[buffer_rows]
            .set(hid_rows.reshape(-1, width_h))
        )
        hid_buf = hid_buf.reshape(ep_count, slots_here, capacity, width_h)
        recv_hid, recv_scaled = (
            lax.all_to_all(hid_buf, "ep", split_axis=0, concat_axis=0, tiled=True),
            lax.all_to_all(scaled_buf, "ep", split_axis=0, concat_axis=0, tiled=True),
        )
        slot_back = jnp.einsum(
            "secd,ehd->sech", recv_scaled, weights, preferred_element_type=jnp.float32
        )
        returned = lax.all_to_all(
            slot_back.astype(jnp.bfloat16), "ep", split_axis=0, concat_axis=0, tiled=True
        )
        partial_value = jnp.einsum(
            "sech,secd->ehd", recv_hid, recv_scaled, preferred_element_type=jnp.float32
        )
        slot_grads = jnp.take(returned.reshape(-1, width_h), buffer_rows, axis=0)
        return (slot_grads.reshape(tok_rows, top_count, width_h), partial_value)

    first_grads, first_partial = expert_pass(
        expert_ids[0], gates[0], hidden[0], cotangent[0], old_place, old_weights
    )
    share_one = lax.psum_scatter(
        first_partial.astype(jnp.bfloat16), "grp", scatter_dimension=2, tiled=True
    )
    got_one = lax.all_to_all(outbound(share_one), "ep", split_axis=0, concat_axis=0, tiled=True)
    second_grads, second_partial = expert_pass(
        expert_ids[1], gates[1], hidden[1], cotangent[1], new_place, new_weights
    )
    share_two = lax.psum_scatter(
        second_partial.astype(jnp.bfloat16), "grp", scatter_dimension=2, tiled=True
    )
    round_two = lax.optimization_barrier(share_two)
    summed = inbound(got_one).astype(jnp.float32) + round_two.astype(jnp.float32)
    expert_grads = (summed / grp_count).astype(jnp.bfloat16)
    slot_grads = jnp.stack([first_grads, second_grads])
    return (slot_grads, new_weights, expert_grads)


def solution(mesh):
    in_specs = (
        P(None, ("grp", "ep"), None),
        P(None, ("grp", "ep"), None),
        P(None, ("grp", "ep"), None, None),
        P(None, ("grp", "ep"), None),
        P(),
        P(),
        P("ep", None, None),
    )
    out_specs = (P(None, ("grp", "ep"), None, None), P("ep", None, None), P("ep", None, "grp"))
    return jax.shard_map(local, mesh=mesh, in_specs=in_specs, out_specs=out_specs, check_vma=False)
```

profile of v0, /device:TPU:2, one launch (start us, length us, event | category | flops | bytes accessed | tf_op | source)
XLA Modules:
  0.0 563.6 jit_solution(5244557788858866819)
XLA Ops:
  7.2 0.8 fusion.54
  8.3 0.9 reduce-window.14
  9.5 0.8 select_reduce_fusion.1
  10.2 2.1 fusion.52
  12.9 3.1 scatter_custom_fusion.2
  16.0 7.5 %all-to-all-start.5 = ((bf16[16,1,32,768]{3,2,1,0:T(8,128)(2,1)}), bf16[16,1,32,768]{3,2,1,0:T(8,128)(2,1)}, u32[]{:S(2)}, u32[]{:S(2)}) async-start(bf16[16,1,32,768]{3,2,1,0:T(8,128)(2,1)} %bitcast.27), calls=%async_computation.5 | async-start | bytes 1572864 | tf_op jit(solution)/shard_map/all_to_all | solution.py:62
  23.9 3.0 mul.89
  26.9 5.0 mul.90
  31.9 5.8 %scatter_custom_fusion = bf16[512,2560]{1,0:T(8,128)(2,1)S(1)} fusion(s32[384]{0:T(512)S(1)} %fusion.50, f32[384,2560]{1,0:T(8,128)} %mul.90, f32[384]{0:T(512)S(1)} %mul.87, bf16[]{:T(256)} %constant.61.clone.1), kind=kCustom, calls=%fused_computation.24 | custom fusion | flops 1966080 | bytes 6555650 | tf_op jit(solution)/shard_map/scatter | solution.py:53
  37.7 38.2 %all_to_all.40 = bf16[16,1,32,2560]{3,2,1,0:T(8,128)(2,1)S(1)} all-to-all(bf16[16,1,32,2560]{3,2,1,0:T(8,128)(2,1)S(1)} %bitcast.154), channel_id=1, replica_groups=mesh['grp'=16,'ep'=16] {'ep'}, dimensions={0} | all-to-all | bytes 5242880 | tf_op jit(solution)/shard_map/all_to_all | solution.py:63
  76.0 1.5 copy-done
  77.4 5.3 fusion
  82.7 16.6 %copy.78 = bf16[1,768,2560]{1,0,2:T(2,128)(2,1)} copy(bf16[1,768,2560]{2,1,0:T(8,128)(2,1)} %fusion) | data formatting | bytes 7864320
  99.3 5.8 %copy.94 = bf16[2560,1,768]{2,0,1:T(8,128)(2,1)} copy(bf16[2560,1,768]{2,1,0:T(2,128)(2,1)} %bitcast.149) | data formatting | bytes 7864320
  105.2 1.2 constant_dynamic-slice_fusion
  107.3 0.6 iota_compare_fusion.6
  107.9 93.7 %reduce-scatter.7.cloned.1.call-done = bf16[160,768]{1,0:T(8,128)(2,1)} async-done(((bf16[2560,768]{1,0:T(8,128)(2,1)}), bf16[160,768]{1,0:T(8,128)(2,1)}) %reduce-scatter.7.cloned.1.call-update) | async-done | bytes 245776
  201.6 1.2 reshape_bitcast_fusion.1
  202.9 3.9 broadcast_select_fusion
  206.8 6.2 %all-to-all-start.2 = ((bf16[16,1,768,160]{2,3,1,0:T(8,128)(2,1)}), bf16[16,1,768,160]{2,3,1,0:T(8,128)(2,1)}, u32[]{:S(2)}, u32[]{:S(2)}) async-start(bf16[16,1,768,160]{2,3,1,0:T(8,128)(2,1)} %get-tuple-element.50), calls=%async_computation.2 | async-start | bytes 7864320 | tf_op jit(solution)/shard_map/all_to_all | solution.py:36
  215.5 50.9 %all-to-all-done.2 = bf16[16,1,768,160]{2,3,1,0:T(8,128)(2,1)} async-done(((bf16[16,1,768,160]{2,3,1,0:T(8,128)(2,1)}), bf16[16,1,768,160]{2,3,1,0:T(8,128)(2,1)}, u32[]{:S(2)}, u32[]{:S(2)}) %all-to-all-start.2) | async-done | bytes 3932192 | tf_op jit(solution)/shard_map/all_to_all | solution.py:36
  266.5 1.7 dynamic-slice_select_fusion
  268.5 0.9 reduce-window.16
  270.4 3.1 scatter_custom_fusion.3
  273.4 5.4 all-to-all-start.7
  279.1 3.0 mul.99
  282.1 5.0 mul.100
  287.1 6.0 %scatter_custom_fusion.1 = bf16[512,2560]{1,0:T(8,128)(2,1)S(1)} fusion(s32[384]{0:T(512)S(1)} %fusion.51, f32[384,2560]{1,0:T(8,128)} %mul.100, f32[384]{0:T(512)S(1)} %mul.97, bf16[]{:T(256)} %constant.61.clone.1), kind=kCustom, calls=%fused_computation.25 | custom fusion | flops 1966080 | bytes 6555650 | tf_op jit(solution)/shard_map/scatter | solution.py:53
  293.1 2.5 all-to-all-done.7
  295.7 51.3 %all_to_all.41 = bf16[16,1,32,2560]{3,2,1,0:T(8,128)(2,1)S(1)} all-to-all(bf16[16,1,32,2560]{3,2,1,0:T(8,128)(2,1)S(1)} %bitcast.153), channel_id=1, replica_groups=mesh['grp'=16,'ep'=16] {'ep'}, dimensions={0} | all-to-all | bytes 5242880 | tf_op jit(solution)/shard_map/all_to_all | solution.py:63
  347.0 1.5 copy-done.2
  348.4 5.3 fusion.1
  353.7 16.6 %copy.80 = bf16[1,768,2560]{1,0,2:T(2,128)(2,1)} copy(bf16[1,768,2560]{2,1,0:T(8,128)(2,1)} %fusion.1) | data formatting | bytes 7864320
  370.3 5.9 %copy.93 = bf16[2560,1,768]{2,0,1:T(8,128)(2,1)} copy(bf16[2560,1,768]{2,1,0:T(2,128)(2,1)} %bitcast.150) | data formatting | bytes 7864320
  376.2 1.7 copy-done.1
  377.9 4.4 fusion.31
  382.3 22.4 %all_to_all.42 = bf16[16,1,32,768]{3,2,1,0:T(8,128)(2,1)S(1)} all-to-all(bf16[16,1,32,768]{3,2,1,0:T(8,128)(2,1)S(1)} %fusion.31), channel_id=1, replica_groups=mesh['grp'=16,'ep'=16] {'ep'}, dimensions={0} | all-to-all | bytes 1572864 | tf_op jit(solution)/shard_map/all_to_all | solution.py:68
  404.7 5.2 all-to-all-start.6
  409.9 6.0 %fusion.26 = bf16[16,1,32,768]{3,2,1,0:T(8,128)(2,1)} fusion(bf16[16,1,32,2560]{3,2,1,0:T(8,128)(2,1)} %copy-done.2, bf16[1,768,2560]{1,2,0:T(8,128)(2,1)} %all-gather.2.cloned.1.call-done), kind=kOutput, calls=%fused_computation.33 | convolution fusion | flops 2013659136 | bytes 7340032 | tf_op jit(solution)/shard_map/secd,ehd->sech/dot_general | solution.py:65
  416.0 59.5 %all-to-all-done.6 = bf16[16,1,768,160]{2,3,1,0:T(8,128)(2,1)} async-done(((bf16[16,1,768,160]{2,3,1,0:T(8,128)(2,1)}), bf16[16,1,768,160]{2,3,1,0:T(8,128)(2,1)}, u32[]{:S(2)}, u32[]{:S(2)}) %all-to-all-start.6) | async-done | bytes 3932192 | tf_op jit(solution)/shard_map/all_to_all | solution.py:83
  475.5 5.7 %all-to-all-start.4 = ((bf16[16,1,32,768]{3,2,1,0:T(8,128)(2,1)}), bf16[16,1,32,768]{3,2,1,0:T(8,128)(2,1)S(1)}, u32[]{:S(2)}, u32[]{:S(2)}) async-start(bf16[16,1,32,768]{3,2,1,0:T(8,128)(2,1)} %fusion.26), calls=%async_computation.4 | async-start | bytes 1572864 | tf_op jit(solution)/shard_map/all_to_all | solution.py:68
  481.2 2.2 gather_fusion
  483.7 59.4 %reduce-scatter.9.cloned.1.call-done = bf16[160,768]{1,0:T(8,128)(2,1)} async-done(((bf16[2560,768]{1,0:T(8,128)(2,1)}), bf16[160,768]{1,0:T(8,128)(2,1)}) %reduce-scatter.9.cloned.1.call-update) | async-done | bytes 245776
  543.1 1.2 reshape_bitcast_fusion
  545.0 1.7 multiply_convert_fusion.4
  546.7 6.3 %copy.69 = bf16[1,768,2560]{2,1,0:T(8,128)(2,1)} copy(bf16[1,768,2560]{1,2,0:T(8,128)(2,1)} %all-gather.2.cloned.1.call-done) | data formatting | bytes 7864320 | tf_op jit(solution)/shard_map/all_gather | solution.py:39
  553.0 2.2 gather_fusion.1
  555.8 1.2 copy.76
  (65 shorter events, 6.4 us)
Async XLA Ops:
  12.4 11.1 %copy-start.5 = (f32[2,64,6]{1,0,2:T(2,128)S(1)}, f32[2,64,6]{1,0,2:T(2,128)}, u32[]{:S(2)}) copy-start(f32[2,64,6]{1,0,2:T(2,128)} %param.12) | copy-start | bytes 9220
  12.4 11.4 %copy-start.4 = (bf16[2,64,2560]{2,1,0:T(8,128)(2,1)S(1)}, bf16[2,64,2560]{2,1,0:T(8,128)(2,1)}, u32[]{:S(2)}) copy-start(bf16[2,64,2560]{2,1,0:T(8,128)(2,1)} %param.14) | copy-start | bytes 1966084
  16.0 21.7 %all-to-all-start.5 = ((bf16[16,1,32,768]{3,2,1,0:T(8,128)(2,1)}), bf16[16,1,32,768]{3,2,1,0:T(8,128)(2,1)}, u32[]{:S(2)}, u32[]{:S(2)}) async-start(bf16[16,1,32,768]{3,2,1,0:T(8,128)(2,1)} %bitcast.27), calls=%async_computation.5 | async-start | bytes 1572864 | tf_op jit(solution)/shard_map/all_to_all | solution.py:62
  23.5 178.1 %reduce-scatter.7.cloned.1.call-start = ((), (), s32[]{:S(2)}) async-start(), calls=%async_computation.11 | async-start | bytes 4177920
  76.0 1.5 copy-start
  105.1 1.4 copy-start.6
  105.1 1.4 copy-start.7
  206.8 62.9 %copy-start.3 = (bf16[1,64,6,768]{3,1,2,0:T(8,128)(2,1)S(1)}, bf16[1,64,6,768]{3,1,2,0:T(8,128)(2,1)}, u32[]{:S(2)}) copy-start(bf16[1,64,6,768]{3,1,2,0:T(8,128)(2,1)} %get-tuple-element.42) | copy-start | bytes 1769476
  206.8 59.7 %all-to-all-start.2 = ((bf16[16,1,768,160]{2,3,1,0:T(8,128)(2,1)}), bf16[16,1,768,160]{2,3,1,0:T(8,128)(2,1)}, u32[]{:S(2)}, u32[]{:S(2)}) async-start(bf16[16,1,768,160]{2,3,1,0:T(8,128)(2,1)} %get-tuple-element.50), calls=%async_computation.2 | async-start | bytes 7864320 | tf_op jit(solution)/shard_map/all_to_all | solution.py:36
  212.9 197.0 %all-gather.2.cloned.1.call-start = ((), (), s32[]{:S(2)}) async-start(), calls=%async_computation.10 | async-start | bytes 4177920 | tf_op jit(solution)/shard_map/all_gather | solution.py:39
  273.4 22.2 %all-to-all-start.7 = ((bf16[16,1,32,768]{3,2,1,0:T(8,128)(2,1)}), bf16[16,1,32,768]{3,2,1,0:T(8,128)(2,1)}, u32[]{:S(2)}, u32[]{:S(2)}) async-start(bf16[16,1,32,768]{3,2,1,0:T(8,128)(2,1)} %bitcast.34), calls=%async_computation.7 | async-start | bytes 1572864 | tf_op jit(solution)/shard_map/all_to_all | solution.py:62
  278.8 264.3 %reduce-scatter.9.cloned.1.call-start = ((), (), s32[]{:S(2)}) async-start(), calls=%async_computation.12 | async-start | bytes 4177920
  347.0 1.5 copy-start.2
  376.2 1.7 copy-start.1
  404.7 70.8 %all-to-all-start.6 = ((bf16[16,1,768,160]{2,3,1,0:T(8,128)(2,1)}), bf16[16,1,768,160]{2,3,1,0:T(8,128)(2,1)}, u32[]{:S(2)}, u32[]{:S(2)}) async-start(bf16[16,1,768,160]{2,3,1,0:T(8,128)(2,1)} %get-tuple-element.49), calls=%async_computation.6 | async-start | bytes 7864320 | tf_op jit(solution)/shard_map/all_to_all | solution.py:83
  475.5 77.5 %all-to-all-start.4 = ((bf16[16,1,32,768]{3,2,1,0:T(8,128)(2,1)}), bf16[16,1,32,768]{3,2,1,0:T(8,128)(2,1)S(1)}, u32[]{:S(2)}, u32[]{:S(2)}) async-start(bf16[16,1,32,768]{3,2,1,0:T(8,128)(2,1)} %fusion.26), calls=%async_computation.4 | async-start | bytes 1572864 | tf_op jit(solution)/shard_map/all_to_all | solution.py:68
Sparse Core Ops, SparseCore 0:
  105.3 96.3 reduce-scatter.6
  268.3 136.8 all-gather.1
  408.5 134.5 reduce-scatter.8
where the time goes:
time: 566 us; the launch traced here: 564 us
  waiting for transfers between devices  266 us (47%)
  blocking collectives  112 us (20%)
  local copies, waits for them, and re-layouts  95.1 us (17%)
  starting transfers between devices  30.1 us (5%)
  other arithmetic  23.3 us (4%)
  matrix products  21 us (4%)
  between operations  16 us (3%)
    unnamed x5, waiting for transfers between devices  153 us
    all_to_all x2, blocking collectives, expert_pass(): lax.all_to_all(scaled_buf, 'ep', split_axis=0, concat_axis=0, tiled=True)  89.5 us
    all_to_all x1, waiting for transfers between devices, local(): lax.all_to_all(outbound(share_one), 'ep', split_axis=0, concat_axis=0, ti...  59.5 us
    unnamed x25, local copies, waits for them, and re-layouts  53.8 us
    all_to_all x1, waiting for transfers between devices, local(): lax.all_to_all(outbound(weight_share), 'ep', split_axis=0, concat_axis=0,...  50.9 us
    all_to_all x1, blocking collectives, expert_pass(): lax.all_to_all(slot_back.astype(jnp.bfloat16), 'ep', split_axis=0, concat...  22.4 us
    mul x6, local copies, waits for them, and re-layouts, expert_pass(): gate_rows[:, :, None] * cot_rows[:, None, :].astype(jnp.float32)  16.3 us
    all_to_all x2, starting transfers between devices, expert_pass(): lax.all_to_all(hid_buf, 'ep', split_axis=0, concat_axis=0, tiled=True)  12.9 us
  transfers between devices with their start and end apart: 8, of which 5 were waited for; matrix products, arithmetic and copies ran while one was open for 16% of the time, Pallas kernels for 0%

commit v1 on v0

v1 whole, which is shorter than its diff:
```python
import jax
import jax.numpy as jnp
from jax import lax
from jax.sharding import PartitionSpec as P

F32 = jnp.float32
BF16 = jnp.bfloat16


def local(expert_ids, gates, hidden, cotangent, old_place, new_place, old_weights):
    ep_count = lax.axis_size("ep")
    grp_count = lax.axis_size("grp")
    width_h, width_d = old_weights.shape[1:]
    experts = old_place.shape[0]
    micros, toks, tops = expert_ids.shape
    cap = min(toks, 32)
    ep_rank = lax.axis_index("ep")
    grp_rank = lax.axis_index("grp")
    share = width_d // grp_count
    numbers = jnp.arange(experts, dtype=jnp.int32)

    eq = expert_ids[..., None] == numbers
    routed = jnp.any(eq, axis=2)
    tri = (jnp.arange(toks)[:, None] > jnp.arange(toks)[None, :]).astype(F32)
    rank = jnp.einsum("tu,mue->mte", tri, routed.astype(F32)).astype(jnp.int32)
    slot_rank = jnp.sum(jnp.where(eq, rank[:, :, None, :], 0), axis=-1)
    row_old = jnp.sum(jnp.where(eq, old_place, 0), axis=-1) * cap + slot_rank
    row_new = jnp.sum(jnp.where(eq, new_place, 0), axis=-1) * cap + slot_rank
    coded = jnp.where(routed, rank, -1).astype(F32)
    at_old = (old_place[:, None] == numbers[None, :]).astype(F32)
    at_new = (new_place[:, None] == numbers[None, :]).astype(F32)
    meta = jnp.concatenate([coded @ at_old, coded @ at_new], axis=-1).astype(BF16)

    my_share = lax.dynamic_slice_in_dim(old_weights[0], grp_rank * share, share, 1).T
    shares = lax.all_gather(my_share, "ep")
    source = jnp.sum(jnp.where(new_place == ep_rank, old_place, 0))
    picked = lax.dynamic_index_in_dim(shares, source, 0, keepdims=False)
    new_weights = lax.all_gather(picked, "grp", tiled=True).T[None]

    gated = (hidden.astype(F32) * gates[..., None]).astype(BF16).reshape(micros, toks * tops, width_h)
    rows = jnp.arange(ep_count * cap)
    put = (rows[None, :, None] == row_new.reshape(micros, 1, -1)).astype(BF16)
    hid_out = jnp.einsum("mrs,msh->mrh", put, gated, preferred_element_type=F32).astype(BF16)
    hid_out = hid_out.reshape(micros, ep_count, cap, width_h).transpose(1, 0, 2, 3)

    meta_all = lax.all_gather(meta, "ep")
    cot_all = lax.all_gather(cotangent, "ep")
    hid_in = lax.all_to_all(hid_out, "ep", split_axis=0, concat_axis=0, tiled=True)

    places = jnp.arange(cap).astype(BF16)
    pick_old = lax.dynamic_index_in_dim(meta_all, ep_rank, 3) == places
    pick_new = lax.dynamic_index_in_dim(meta_all, experts + ep_rank, 3) == places
    hid_rows = jnp.einsum(
        "smtp,smph->smth", pick_new.astype(BF16), hid_in, preferred_element_type=F32
    ).astype(BF16)
    cot_rows = cot_all.reshape(-1, width_d)
    part = lax.dot_general(
        cot_rows, hid_rows.reshape(-1, width_h), (((0,), (0,)), ((), ())), preferred_element_type=F32
    ).astype(BF16)
    summed = lax.psum_scatter(part, "grp", scatter_dimension=0, tiled=True)

    back = lax.dot_general(
        cot_rows, old_weights[0], (((1,), (1,)), ((), ())), preferred_element_type=F32
    ).astype(BF16)
    back = jnp.einsum(
        "smtp,smth->smph",
        pick_old.astype(BF16),
        back.reshape(ep_count, micros, toks, width_h),
        preferred_element_type=F32,
    ).astype(BF16)
    returned = lax.all_to_all(back, "ep", split_axis=0, concat_axis=0, tiled=True)
    returned = returned.transpose(1, 0, 2, 3).reshape(micros, ep_count * cap, width_h)
    get = (rows[None, None, :] == row_old.reshape(micros, -1, 1)).astype(BF16)
    got = jnp.einsum("msr,mrh->msh", get, returned, preferred_element_type=F32)
    slot_grads = (got.reshape(micros, toks, tops, width_h) * gates[..., None]).astype(BF16)

    expert_grads = (summed.astype(F32) / grp_count).astype(BF16).T[None]
    return slot_grads, new_weights, expert_grads


def solution(mesh):
    in_specs = (
        P(None, ("grp", "ep"), None),
        P(None, ("grp", "ep"), None),
        P(None, ("grp", "ep"), None, None),
        P(None, ("grp", "ep"), None),
        P(),
        P(),
        P("ep", None, None),
    )
    out_specs = (P(None, ("grp", "ep"), None, None), P("ep", None, None), P("ep", None, "grp"))
    return jax.shard_map(local, mesh=mesh, in_specs=in_specs, out_specs=out_specs, check_vma=False)
```

time: 566 us -> 398 us (0.70)
  blocking collectives: 112 us -> 22.1 us
  local copies, waits for them, and re-layouts: 95.1 us -> 23.4 us
  waiting for transfers between devices: 266 us -> 290 us
  other arithmetic: 23.3 us -> 4.24 us
  starting transfers between devices: 30.1 us -> 11.3 us
  matrix products: 21 us -> 30.5 us
    all_gather x1 -> x3, waiting for transfers between devices: 0.02 us -> 140 us  [the longest x1 85.5 us: local(): cot_all = lax.all_gather(cotangent, 'ep')]
    all_to_all x3 -> x0, blocking collectives: 112 us -> none  [the longest x2 89.5 us: expert_pass(): lax.all_to_all(scaled_buf, 'ep', split_axis=0, concat_axis=0, tiled=True)]
    unnamed x5, waiting for transfers between devices: 153 us -> 90.7 us
    all_to_all x5 -> x2, waiting for transfers between devices: 113 us -> 59.1 us  [the longest x1 30.3 us: local(): lax.all_to_all(back, 'ep', split_axis=0, concat_axis=0, tiled=True)]
    unnamed x25 -> x19, local copies, waits for them, and re-layouts: 53.8 us -> 15.9 us
    all_gather x0 -> x1, blocking collectives: none -> 22.1 us  [local(): meta_all = lax.all_gather(meta, 'ep')]
    all_to_all x5 -> x2, starting transfers between devices: 30 us -> 10.9 us  [the longest x1 5.48 us: local(): lax.all_to_all(hid_out, 'ep', split_axis=0, concat_axis=0, tiled=True)]
    mul x6 -> x0, local copies, waits for them, and re-layouts: 16.3 us -> none  [expert_pass(): gate_rows[:, :, None] * cot_rows[:, None, :].astype(jnp.float32)]
  transfers between devices with their start and end apart: 8 -> 6, of which waited for: 5 -> 6; matrix products, arithmetic and copies ran while one was open for 16% -> 14% of each run, Pallas kernels for 0% -> 0%
where the time goes in v1:
time: 398 us; the launch traced here: 397 us
  waiting for transfers between devices  290 us (73%)
  matrix products  30.5 us (8%)
  local copies, waits for them, and re-layouts  23.4 us (6%)
  blocking collectives  22.1 us (6%)
  between operations  16 us (4%)
  starting transfers between devices  11.3 us (3%)
  other arithmetic  4.24 us (1%)
    unnamed x5, waiting for transfers between devices  90.7 us
    all_gather x1, waiting for transfers between devices, local(): cot_all = lax.all_gather(cotangent, 'ep')  85.5 us
    all_gather x1, waiting for transfers between devices, local(): shares = lax.all_gather(my_share, 'ep')  38.3 us
    all_to_all x1, waiting for transfers between devices, local(): lax.all_to_all(back, 'ep', split_axis=0, concat_axis=0, tiled=True)  30.3 us
    all_to_all x1, waiting for transfers between devices, local(): lax.all_to_all(hid_out, 'ep', split_axis=0, concat_axis=0, tiled=True)  28.8 us
    all_gather x1, blocking collectives, local(): meta_all = lax.all_gather(meta, 'ep')  22.1 us
    all_gather x1, waiting for transfers between devices, local(): new_weights = lax.all_gather(picked, 'grp', tiled=True).T[None]  16.3 us
    unnamed x19, local copies, waits for them, and re-layouts  15.9 us
  transfers between devices with their start and end apart: 6, of which 6 were waited for; matrix products, arithmetic and copies ran while one was open for 14% of the time, Pallas kernels for 0%

profile of v1, /device:TPU:2, one launch (start us, length us, event | category | flops | bytes accessed | tf_op | source)
XLA Modules:
  0.0 397.4 jit_solution(9279935929328025857)
XLA Ops:
  7.2 0.0 copy-start.4
  7.2 0.0 copy-start.3
  7.2 0.0 all-gather.9.cloned.1.call-start
  7.2 1.2 constant_dynamic-slice_fusion.2
  8.5 0.8 copy.53
  9.3 0.0 all-gather.9.cloned.1.call-update
  9.4 0.0 all-gather.7.cloned.1.call-start
  9.4 0.7 all-gather.7.cloned.1.call-update
  10.1 0.0 all-gather.11.cloned.1.call-start
  10.2 1.3 fusion.41
  12.8 0.1 fusion.11
  13.0 0.1 fusion.12
  13.1 0.1 fusion.13
  13.2 22.1 %all_gather.19 = bf16[16,2,64,32]{2,3,1,0:T(8,128)(2,1)S(1)} all-gather(bf16[1,2,64,32]{2,3,1,0:T(8,128)(2,1)S(1)} %pad_maximum_fusion), channel_id=1, replica_groups=mesh['grp'=16,'ep'=16] {'ep'}, dimensions={0}, use_global_device_ids=true | all-gather | bytes 139264 | tf_op jit(solution)/shard_map/all_gather | solution.py:46
  36.1 38.3 %all-gather.9.cloned.1.call-done = bf16[2560,768]{1,0:T(8,128)(2,1)} async-done(((bf16[160,768]{1,0:T(8,128)(2,1)}), bf16[2560,768]{1,0:T(8,128)(2,1)}) %all-gather.9.cloned.1.call-update) | async-done | bytes 3932176 | tf_op jit(solution)/shard_map/all_gather | solution.py:35
  74.4 1.7 constant_dynamic-slice_fusion.1
  76.1 0.0 all-gather.11.cloned.1.call-update
  76.1 85.5 %all-gather.7.cloned.1.call-done = bf16[32,64,2560]{2,1,0:T(8,128)(2,1)} async-done(((bf16[2,64,2560]{2,1,0:T(8,128)(2,1)}), bf16[32,64,2560]{2,1,0:T(8,128)(2,1)}) %all-gather.7.cloned.1.call-update) | async-done | bytes 10485776 | tf_op jit(solution)/shard_map/all_gather | solution.py:47
  161.6 12.2 %fusion.3 = bf16[2048,768]{1,0:T(8,128)(2,1)S(1)} fusion(bf16[2048,2560]{1,0:T(8,128)(2,1)} %bitcast.76, bf16[1,768,2560]{2,1,0:T(8,128)(2,1)} %param.13), kind=kOutput, calls=%fused_computation.4 | convolution fusion | flops 8054636544 | bytes 17563648 | tf_op jit(solution)/shard_map/dot_general | solution.py:62
  173.8 1.8 convolution_convert_fusion.1
  175.6 5.5 %all-to-all-start = ((bf16[16,2,32,768]{3,2,1,0:T(8,128)(2,1)}), bf16[16,2,32,768]{3,2,1,0:T(8,128)(2,1)S(1)}, u32[]{:S(2)}, u32[]{:S(2)}) async-start(bf16[16,2,32,768]{3,2,1,0:T(8,128)(2,1)} %convolution_convert_fusion.1), calls=%async_computation | async-start | bytes 3145728 | tf_op jit(solution)/shard_map/all_to_all | solution.py:71
  181.1 0.1 select_reduce_fusion
  181.2 0.1 copy.47
  181.3 0.1 add.39
  181.4 0.2 copy.52
  181.6 0.1 copy.56
  181.7 0.1 add.45
  181.9 30.3 %all-to-all-done = bf16[16,2,32,768]{3,2,1,0:T(8,128)(2,1)S(1)} async-done(((bf16[16,2,32,768]{3,2,1,0:T(8,128)(2,1)}), bf16[16,2,32,768]{3,2,1,0:T(8,128)(2,1)S(1)}, u32[]{:S(2)}, u32[]{:S(2)}) %all-to-all-start) | async-done | bytes 1572896 | tf_op jit(solution)/shard_map/all_to_all | solution.py:71
  212.1 0.1 copy.50
  212.3 0.8 fusion.9
  213.1 0.0 copy-start
  213.1 1.8 copy.51
  214.9 2.7 multiply_convert_fusion
  217.6 1.0 convolution_convert_fusion
  218.6 1.3 copy.74
  219.9 5.5 %all-to-all-start.1 = ((bf16[16,2,32,768]{3,2,1,0:T(8,128)(2,1)}), bf16[16,2,32,768]{3,2,1,0:T(8,128)(2,1)S(1)}, u32[]{:S(2)}, u32[]{:S(2)}) async-start(bf16[16,2,32,768]{3,2,1,0:T(8,128)(2,1)} %bitcast.62), calls=%async_computation.1 | async-start | bytes 3145728 | tf_op jit(solution)/shard_map/all_to_all | solution.py:48
  225.4 0.2 reduce-scatter.4.cloned.1.call-start
  225.6 28.8 %all-to-all-done.1 = bf16[16,2,32,768]{3,2,1,0:T(8,128)(2,1)S(1)} async-done(((bf16[16,2,32,768]{3,2,1,0:T(8,128)(2,1)}), bf16[16,2,32,768]{3,2,1,0:T(8,128)(2,1)S(1)}, u32[]{:S(2)}, u32[]{:S(2)}) %all-to-all-start.1) | async-done | bytes 1572896 | tf_op jit(solution)/shard_map/all_to_all | solution.py:48
  254.5 14.3 %fusion = bf16[2560,768]{0,1:T(8,128)(2,1)} fusion(bf16[16,2,64,2560]{3,2,1,0:T(8,128)(2,1)} %bitcast.77, bf16[16,2,32,768]{3,2,1,0:T(8,128)(2,1)S(1)} %all-to-all-done.1, bf16[16,2,64]{2,1,0:T(2,128)(2,1)S(1)} %copy.55, bf16[32]{0:T(256)(128)(2,1)S(1)} %iota_convert_fusion), kind=kOutput, calls=%fused_computation.1 | convolution fusion | flops 8157331456 | bytes 15994944 | tf_op jit(solution)/shard_map/dot_general | solution.py:57
  268.8 6.3 %copy.64 = bf16[2560,768]{1,0:T(8,128)(2,1)} copy(bf16[2560,768]{0,1:T(8,128)(2,1)} %fusion) | data formatting | bytes 7864320
  275.1 0.0 reduce-scatter.4.cloned.1.call-update
  275.1 16.3 %all-gather.11.cloned.1.call-done = bf16[1,2560,768]{2,1,0:T(8,128)(2,1)} async-done(((bf16[1,160,768]{2,1,0:T(8,128)(2,1)}), bf16[1,2560,768]{2,1,0:T(8,128)(2,1)}) %all-gather.11.cloned.1.call-update) | async-done | bytes 3932176 | tf_op jit(solution)/shard_map/all_gather | solution.py:38
  291.4 6.3 %copy.61 = bf16[1,768,2560]{2,1,0:T(8,128)(2,1)} copy(bf16[1,768,2560]{1,2,0:T(8,128)(2,1)} %bitcast.68) | data formatting | bytes 7864320
  297.7 1.2 copy.60
  298.8 90.0 %reduce-scatter.4.cloned.1.call-done = bf16[160,768]{1,0:T(8,128)(2,1)} async-done(((bf16[2560,768]{1,0:T(8,128)(2,1)}), bf16[160,768]{1,0:T(8,128)(2,1)}) %reduce-scatter.4.cloned.1.call-update) | async-done | bytes 245776
  388.8 1.1 copy.65
  389.9 0.1 fusion.19
  390.0 0.8 copy.62
  (17 shorter events, 0.1 us)
Async XLA Ops:
  7.2 5.8 %copy-start.4 = (s32[16]{0:T(128)S(1)}, s32[16]{0:T(128)}, u32[]{:S(2)}) copy-start(s32[16]{0:T(128)} %param.11) | copy-start | bytes 196
  7.2 5.9 %copy-start.3 = (s32[16]{0:T(128)S(1)}, s32[16]{0:T(128)}, u32[]{:S(2)}) copy-start(s32[16]{0:T(128)} %param.12) | copy-start | bytes 196
  7.2 5.6 %copy-start.1 = (s32[2,64,6]{1,0,2:T(2,128)S(1)}, s32[2,64,6]{1,0,2:T(2,128)}, u32[]{:S(2)}) copy-start(s32[2,64,6]{1,0,2:T(2,128)} %param.7) | copy-start | bytes 9220
  7.2 67.2 %all-gather.9.cloned.1.call-start = ((), (), s32[]{:S(2)}) async-start(), calls=%async_computation.4 | async-start | bytes 4177920 | tf_op jit(solution)/shard_map/all_gather | solution.py:35
  9.4 152.2 %all-gather.7.cloned.1.call-start = ((), (), s32[]{:S(2)}) async-start(), calls=%async_computation.3 | async-start | bytes 11141120 | tf_op jit(solution)/shard_map/all_gather | solution.py:47
  10.1 281.3 %all-gather.11.cloned.1.call-start = ((), (), s32[]{:S(2)}) async-start(), calls=%async_computation.5 | async-start | bytes 4177920 | tf_op jit(solution)/shard_map/all_gather | solution.py:38
  175.6 5.8 %copy-start.2 = (f32[2,64,6]{1,0,2:T(2,128)S(1)}, f32[2,64,6]{1,0,2:T(2,128)}, u32[]{:S(2)}) copy-start(f32[2,64,6]{1,0,2:T(2,128)} %param.8) | copy-start | bytes 9220
  175.6 36.5 %all-to-all-start = ((bf16[16,2,32,768]{3,2,1,0:T(8,128)(2,1)}), bf16[16,2,32,768]{3,2,1,0:T(8,128)(2,1)S(1)}, u32[]{:S(2)}, u32[]{:S(2)}) async-start(bf16[16,2,32,768]{3,2,1,0:T(8,128)(2,1)} %convolution_convert_fusion.1), calls=%async_computation | async-start | bytes 3145728 | tf_op jit(solution)/shard_map/all_to_all | solution.py:71
  213.1 1.8 copy-start
  219.9 34.6 %all-to-all-start.1 = ((bf16[16,2,32,768]{3,2,1,0:T(8,128)(2,1)}), bf16[16,2,32,768]{3,2,1,0:T(8,128)(2,1)S(1)}, u32[]{:S(2)}, u32[]{:S(2)}) async-start(bf16[16,2,32,768]{3,2,1,0:T(8,128)(2,1)} %bitcast.62), calls=%async_computation.1 | async-start | bytes 3145728 | tf_op jit(solution)/shard_map/all_to_all | solution.py:48
  225.4 163.4 %reduce-scatter.4.cloned.1.call-start = ((), (), s32[]{:S(2)}) async-start(), calls=%async_computation.6 | async-start | bytes 4177920
Sparse Core Ops, SparseCore 0:
  11.3 63.0 all-gather.8
  77.1 84.4 all-gather.6
  164.0 127.3 all-gather.10
  293.8 94.9 reduce-scatter.3

commit v2 on v1

v2 whole, which is shorter than its diff:
```python
import functools

import jax
import jax.numpy as jnp
from jax import lax
from jax.experimental import pallas as pl
from jax.experimental.pallas import tpu as pltpu
from jax.sharding import PartitionSpec as P

F32 = jnp.float32
BF16 = jnp.bfloat16
MESH = pl.DeviceIdType.MESH

CHUNKS = 5
PIECES = 17
CAP = 32


def dot(a, b, ca, cb):
    return lax.dot_general(a, b, (((ca,), (cb,)), ((), ())), preferred_element_type=F32)


def kernel(
    ids, gates, old_place, new_place, hid, cot, w_old, sg_out, w_out, eg_out,
    gat, wsh, w_res, w_perm, cot_v, hid_v, a_mat, hid_send, hid_in, hid_rows, acc,
    meta_send, meta_in, ret_send, ret_in, part, rs_r0, rs_l0, rs_r, rs_l, ysend, yrecv, eg_sum,
    w_own, sg_v,
    loc, ag_s, ag_r, hid_s, hid_r, meta_s, meta_r, ret_s, ret_r, z_s, z_r, zy_s, zy_r, c_s, c_r, cy_s, cy_r,
):
    g = lax.axis_index("grp")
    me = lax.axis_index("ep")
    z, yl = g // 2, g % 2
    core, xx, yh = me % 2, (me // 2) % 4, me // 8
    share = w_own.shape[0]
    ep_n = 16
    width_h = hid_v.shape[-1]

    def at_ep(dy=0, dx=0, dc=0):
        return (((yh + dy) % 2) * 4 + (xx + dx + 4) % 4) * 2 + (core + dc) % 2

    def to_ep(e):
        return (g, e)

    zp, zm = (((z + 1) % 8) * 2 + yl, me), (((z + 7) % 8) * 2 + yl, me)
    yp = (z * 2 + 1 - yl, me)
    left, right, yside, other = at_ep(dx=-1), at_ep(dx=1), at_ep(dy=1), at_ep(dc=1)

    def rdma(src, dst, ss, rs, dev):
        return pltpu.make_async_remote_copy(
            src_ref=src, dst_ref=dst, send_sem=ss, recv_sem=rs, device_id=dev, device_id_type=MESH
        )

    barrier = pltpu.get_barrier_semaphore()
    for d in range(1, ep_n):
        pl.semaphore_signal(barrier, 1, device_id=to_ep((me + d) % ep_n), device_id_type=MESH)
    for dev in (zp, zm, yp):
        pl.semaphore_signal(barrier, 1, device_id=dev, device_id_type=MESH)

    loads = [pltpu.make_async_copy(cot, cot_v, loc.at[0]), pltpu.make_async_copy(w_old, w_res, loc.at[1])]
    loads += [pltpu.make_async_copy(hid.at[:, k], hid_v.at[k], loc.at[2 + k]) for k in range(6)]
    my_rows = pl.ds(pl.multiple_of(g * share, 16), share)
    loads.append(pltpu.make_async_copy(w_old.at[my_rows], wsh.at[me], loc.at[8]))
    for cp in loads:
        cp.start()
    pl.semaphore_wait(barrier, ep_n - 1 + 3)

    def block(job, src):
        if job is None:
            return wsh.at[src]
        return gat.at[job, src]

    def half(job, src, h):
        if job is None:
            n = wsh.shape[2] // 2
            return wsh.at[src, :, pl.ds(h * n, n)]
        n = gat.shape[2] // 2
        return gat.at[job, src, pl.ds(h * n, n)]

    def ag_send(job, piece, ref, dev, src=None):
        j = 0 if job is None else job + 1
        rdma(ref if src is None else src, ref, ag_s.at[j, piece], ag_r.at[j, piece], to_ep(dev)).start()

    def ag_wait(job, piece, ref):
        j = 0 if job is None else job + 1
        rdma(ref, ref, ag_s.at[j, piece], ag_r.at[j, piece], to_ep(other)).wait_recv()

    def ag0(job):
        own = block(job, me)
        src = w_old.at[my_rows] if job is None else None
        ag_send(job, 0, own, right, src)
        ag_send(job, 1, own, left, src)
        ag_send(job, 2, own, yside, src)
        ag_send(job, 3, own, other, src)

    x2 = at_ep(dx=2)
    yleft, yright, yx2 = at_ep(dy=1, dx=-1), at_ep(dy=1, dx=1), at_ep(dy=1, dx=2)

    def ag1(job):
        ag_wait(job, 0, block(job, left))
        ag_send(job, 4, half(job, left, 0), right)
        ag_send(job, 10, block(job, left), other)
        ag_wait(job, 1, block(job, right))
        ag_send(job, 5, half(job, right, 1), left)
        ag_send(job, 11, block(job, right), other)
        ag_wait(job, 2, block(job, yside))
        ag_send(job, 6, block(job, yside), right)
        ag_send(job, 7, block(job, yside), left)
        ag_send(job, 12, block(job, yside), other)

    def ag2(job):
        ag_wait(job, 4, half(job, x2, 0))
        ag_send(job, 8, half(job, x2, 0), yside)
        ag_wait(job, 5, half(job, x2, 1))
        ag_send(job, 9, half(job, x2, 1), yside)
        ag_send(job, 13, block(job, x2), other)
        ag_wait(job, 6, block(job, yleft))
        ag_send(job, 14, block(job, yleft), other)
        ag_wait(job, 7, block(job, yright))
        ag_send(job, 15, block(job, yright), other)

    def ag3(job):
        ag_wait(job, 8, half(job, yx2, 0))
        ag_wait(job, 9, half(job, yx2, 1))
        ag_send(job, 16, block(job, yx2), other)

    def across(e):
        return (e // 2) * 2 + 1 - core

    def ag4(job):
        for piece, src in ((3, me), (10, left), (11, right), (12, yside), (13, x2), (14, yleft), (15, yright), (16, yx2)):
            ag_wait(job, piece, block(job, across(src)))

    def ag_drain(job):
        for piece in range(PIECES):
            ref = half(job, me, 0) if piece in (4, 5, 8, 9) else block(job, me)
            j = 0 if job is None else job + 1
            rdma(ref, ref, ag_s.at[j, piece], ag_r.at[j, piece], to_ep(other)).wait_send()

    ag0(None)

    lane = lax.broadcasted_iota(jnp.int32, (16, 128), 1)
    row16 = lax.broadcasted_iota(jnp.int32, (16, 128), 0)
    micro = (lane[:1] >= 64).astype(F32)
    ui = lax.broadcasted_iota(jnp.int32, (128, 128), 0)
    uj = lax.broadcasted_iota(jnp.int32, (128, 128), 1)
    upper = ((ui < uj) & ((ui >= 64) == (uj >= 64))).astype(BF16)
    slot_of = [jnp.zeros((16, 128), F32), jnp.zeros((16, 128), F32)]
    source = jnp.int32(0)
    for e in range(16):
        slot_of[0] = jnp.where(row16 == e, old_place[e].astype(F32), slot_of[0])
        slot_of[1] = jnp.where(row16 == e, new_place[e].astype(F32), slot_of[1])
        source = source + jnp.where(new_place[e] == me, old_place[e], 0)
    target = [[], []]
    for which in (0, 1):
        slots, hits = [], []
        for k in range(6):
            eq = ids[k : k + 1, :] == row16
            slot = jnp.sum(jnp.where(eq, slot_of[which], 0.0), axis=0, keepdims=True)
            slots.append(slot)
            hits.append(row16.astype(F32) == slot)
        routed = sum(h.astype(F32) for h in hits)
        rank = dot(routed.astype(BF16), upper, 1, 0)
        for k in range(6):
            mine = jnp.sum(jnp.where(hits[k], rank, 0.0), axis=0, keepdims=True)
            target[which].append(slots[k] * (2 * CAP) + micro * CAP + mine)
        coded = jnp.where(routed > 0.5, rank + micro * CAP, -1.0)
        for s in range(16):
            meta_send[s, which : which + 1, :] = coded[s : s + 1, :]

    def build(which):
        rows = lax.broadcasted_iota(jnp.int32, (1024, 128), 0).astype(F32)
        for k in range(6):
            a_mat[:, k * 128 : (k + 1) * 128] = jnp.where(
                rows == target[which][k], gates[k : k + 1, :], 0.0
            ).astype(BF16)

    def spread_out(src, dst, ss, rs):
        for d in range(1, ep_n):
            e = (me + d) % ep_n
            rdma(src.at[e], dst.at[me], ss.at[d], rs.at[d], to_ep(e)).start()

    def spread_wait(dst, ss, rs):
        for d in range(1, ep_n):
            e = (me - d + ep_n) % ep_n
            rdma(dst.at[e], dst.at[e], ss.at[d], rs.at[d], to_ep(other)).wait_recv()

    def spread_drain(src, ss, rs):
        for d in range(1, ep_n):
            rdma(src.at[me], src.at[me], ss.at[d], rs.at[d], to_ep(other)).wait_send()

    spread_out(meta_send, meta_in, meta_s, meta_r)
    meta_in[me] = meta_send[me]

    build(1)
    for cp in loads[2:8]:
        cp.wait()
    hid_all = hid_v[...].reshape(6 * 128, width_h)

    def pack(i, _):
        rows = pl.ds(pl.multiple_of(i * 256, 256), 256)
        res = dot(a_mat[rows, :], hid_v[...].reshape(6 * 128, width_h), 1, 0).astype(BF16)
        hid_send[pl.ds(i * 4, 4)] = res.reshape(4, 64, width_h)
        return 0

    lax.fori_loop(0, 4, pack, 0)
    spread_out(hid_send, hid_in, hid_s, hid_r)
    hid_in[me] = hid_send[me]

    def chooser(c):
        i = lax.broadcasted_iota(jnp.int32, (640, 128), 0)
        j = lax.broadcasted_iota(jnp.int32, (640, 128), 1)
        return (i == (j // 32) * 160 + c * 32 + j % 32).astype(BF16)

    loads[0].wait()

    def perm_cot(c, _):
        sel = chooser(c)
        for q in range(4):
            gat[c, me, :, q * 128 : (q + 1) * 128] = dot(
                cot_v[:, q * 640 : (q + 1) * 640], sel, 1, 0
            ).astype(BF16)
        return 0

    lax.fori_loop(0, CHUNKS, perm_cot, 0)
    ag0(0)
    ag1(None)
    loads[1].wait()

    def perm_w(c, _):
        sel = chooser(c)
        for q in range(4):
            w_perm[c, :, q * 128 : (q + 1) * 128] = dot(
                w_res[:, q * 640 : (q + 1) * 640], sel, 1, 0
            ).astype(BF16)
        return 0

    lax.fori_loop(0, 2, perm_w, 0)
    ag2(None)
    lax.fori_loop(2, CHUNKS, perm_w, 0)
    ag3(None)
    loads[8].wait()
    ag4(None)

    def w_rows(zz, yy):
        return w_out.at[pl.ds(pl.multiple_of(((zz + 16) % 8 * 2 + yy) * share, 16), share)]

    def z_send(ref, dst, way, step, yy):
        rdma(ref, dst, z_s.at[way, step, yy], z_r.at[way, step, yy], zp if way == 0 else zm).start()

    def z_wait(ref, way, step, yy):
        rdma(ref, ref, z_s.at[way, step, yy], z_r.at[way, step, yy], zp).wait_recv()

    w_own[...] = wsh[source]
    keep_own = pltpu.make_async_copy(w_own, w_rows(z, yl), loc.at[9])
    keep_own.start()
    for way in (0, 1):
        z_send(w_own, w_rows(z, yl), way, 0, yl)
    rdma(w_own, w_rows(z, yl), zy_s.at[0], zy_r.at[0], yp).start()

    def zag(step):
        if step == 0:
            ref = w_rows(z, 1 - yl)
            rdma(ref, ref, zy_s.at[0], zy_r.at[0], yp).wait_recv()
            for way in (0, 1):
                z_send(ref, ref, way, 0, 1 - yl)
            return
        for way in (0, 1):
            zz = z - step if way == 0 else z + step
            for yy in (0, 1):
                ref = w_rows(zz, yy)
                if step < 4 or yy == way:
                    z_wait(ref, way, step - 1, yy)
                if step < 3 or (step == 3 and yy == way):
                    z_send(ref, ref, way, step, yy)

    def c_rows(c, zz, h=None):
        start = pl.multiple_of(((zz + 16) % 8) * 64 + (0 if h is None else h * 32), 32)
        return part.at[c, pl.ds(start, 64 if h is None else 32)]

    def add_into(ref, other_ref):
        ref[...] = (ref[...].astype(F32) + other_ref[...].astype(F32)).astype(BF16)

    def rs_move(c, step, way, src, dst):
        return rdma(src, dst, c_s.at[c, step, way], c_r.at[c, step, way], zp if way == 0 else zm)

    def rs(c, step):
        if step == 0:
            rs_move(c, 0, 0, c_rows(c, z + 4, 0), rs_r0.at[c]).start()
            rs_move(c, 0, 1, c_rows(c, z - 4, 1), rs_l0.at[c]).start()
            return
        if step == 5:
            rdma(yrecv.at[c], yrecv.at[c], cy_s.at[c], cy_r.at[c], yp).wait_recv()
            tot = eg_sum[c] + yrecv[c].astype(F32)
            eg_out[pl.ds(pl.multiple_of(c * 32, 32), 32), :] = (tot / 16.0).astype(BF16)
            return
        if step == 4:
            rs_move(c, 3, 0, rs_r.at[c, 2], rs_r.at[c, 2]).wait_recv()
            rs_move(c, 3, 1, rs_l.at[c, 2], rs_l.at[c, 2]).wait_recv()
            for h in (0, 1):
                rows = pl.ds(h * 32, 32)
                tot = (
                    c_rows(c, z, h)[...].astype(F32)
                    + rs_r[c, 2, rows, :].astype(F32)
                    + rs_l[c, 2, rows, :].astype(F32)
                )

                @pl.when(yl == h)
                def _():
                    eg_sum[c] = tot

                @pl.when(yl != h)
                def _():
                    ysend[c] = tot.astype(BF16)

            rdma(ysend.at[c], yrecv.at[c], cy_s.at[c], cy_r.at[c], yp).start()
            return
        for way, first, later in ((0, rs_r0, rs_r), (1, rs_l0, rs_l)):
            tgt = z + 4 - step if way == 0 else z - 4 + step
            if step == 1:
                rs_move(c, 0, way, first.at[c], first.at[c]).wait_recv()
                add_into(c_rows(c, tgt, way), first.at[c])
            else:
                rs_move(c, step - 1, way, later.at[c, step - 2], later.at[c, step - 2]).wait_recv()
                add_into(c_rows(c, tgt), later.at[c, step - 2])
            rs_move(c, step, way, c_rows(c, tgt), later.at[c, step - 1]).start()

    def rs_drain(c):
        for way in (0, 1):
            rs_move(c, 0, way, rs_r0.at[c], rs_r0.at[c]).wait_send()
            for step in (1, 2, 3):
                rs_move(c, step, way, rs_r.at[c, 0], rs_r.at[c, 0]).wait_send()
        rdma(ysend.at[c], ysend.at[c], cy_s.at[c], cy_r.at[c], yp).wait_send()

    acc[...] = jnp.zeros_like(acc)
    zag(0)
    spread_wait(meta_in, meta_s, meta_r)
    spread_wait(hid_in, hid_s, hid_r)
    code_row = lax.broadcasted_iota(jnp.int32, (64, 128), 0).astype(F32)

    def place_rows(s, _):
        sel = (code_row == meta_in[s, 1:2, :]).astype(BF16)
        hid_rows[s] = dot(sel, hid_in[s], 0, 0).astype(BF16)
        return 0

    lax.fori_loop(0, ep_n, place_rows, 0)

    def back(c, lo, hi):
        def body(i, _):
            rows = pl.ds(i * 4, 4)
            res = dot(gat[c, rows].reshape(512, 512), w_perm[c], 1, 1)
            acc[rows] += res.reshape(4, 128, width_h)
            return 0

        lax.fori_loop(lo, hi, body, 0)

    def weight_part(c):
        def body(n, _):
            cols = pl.ds(pl.multiple_of(n * 256, 256), 256)
            left_rows = gat[c].reshape(ep_n * 128, 512)
            right_rows = hid_rows[:, :, cols].reshape(ep_n * 128, 256)
            part[c, :, cols] = dot(left_rows, right_rows, 0, 0).astype(BF16)
            return 0

        lax.fori_loop(0, width_h // 256, body, 0)

    def inside(c, f):
        pl.when((c >= 0) & (c < CHUNKS))(lambda: f(c))

    def sums(i):
        for step in (5, 4, 3, 2, 1):
            inside(i - 3 - step, lambda c: rs(c, step))

    def tick(i, _):
        inside(i + 1, ag0)
        inside(i, ag1)
        inside(i - 3, ag4)
        inside(i - 3, lambda c: back(c, 0, 2))
        inside(i - 1, ag2)
        inside(i - 3, lambda c: back(c, 2, 4))
        inside(i - 2, ag3)
        for step in range(1, 5):
            pl.when(i == 2 * step - 1)(lambda: zag(step))
        inside(i - 3, weight_part)
        inside(i - 3, lambda c: rs(c, 0))
        sums(i)
        return 0

    lax.fori_loop(0, CHUNKS + 3, tick, 0)

    def send_back(s, _):
        sel = (code_row == meta_in[s, 0:1, :]).astype(BF16)
        ret_send[s] = dot(sel, acc[s].astype(BF16), 1, 0).astype(BF16)
        return 0

    lax.fori_loop(0, ep_n, send_back, 0)
    spread_out(ret_send, ret_in, ret_s, ret_r)
    ret_in[me] = ret_send[me]
    build(0)

    def tail(i, _):
        sums(i)
        return 0

    lax.fori_loop(CHUNKS + 3, CHUNKS + 8, tail, 0)
    spread_wait(ret_in, ret_s, ret_r)

    def take(k):
        cols = slice(k * 128, (k + 1) * 128)
        sg_v[k] = dot(a_mat[:, cols], ret_in[...].reshape(1024, width_h), 0, 0).astype(BF16)

    outs = []
    for k in range(6):
        take(k)
        for m in (0, 1):
            cp = pltpu.make_async_copy(sg_v.at[k, pl.ds(m * 64, 64)], sg_out.at[m, k], loc.at[10 + 2 * k + m])
            cp.start()
            outs.append(cp)

    ag_drain(None)

    def drain(c, _):
        ag_drain(c)
        rs_drain(c)
        return 0

    lax.fori_loop(0, CHUNKS, drain, 0)
    spread_drain(meta_send, meta_s, meta_r)
    spread_drain(hid_send, hid_s, hid_r)
    spread_drain(ret_send, ret_s, ret_r)
    keep_own.wait()
    rdma(w_own, w_own, zy_s.at[0], zy_r.at[0], yp).wait_send()
    for way in (0, 1):
        for step in range(4):
            for yy in (0, 1):
                if step < 3 or yy == way:
                    rdma(w_own, w_own, z_s.at[way, step, yy], z_r.at[way, step, yy], yp).wait_send()
    for cp in outs:
        cp.wait()


def local(expert_ids, gates, hidden, cotangent, old_place, new_place, old_weights):
    micros, toks, tops = expert_ids.shape
    width_h, width_d = old_weights.shape[1:]
    lanes = micros * toks
    share = width_h // 16
    out_rows = width_d // 16
    ids_t = expert_ids.transpose(2, 0, 1).reshape(tops, lanes)
    gates_t = gates.transpose(2, 0, 1).reshape(tops, lanes)
    hid_t = hidden.transpose(0, 2, 1, 3)
    cot = cotangent.reshape(lanes, width_d)
    vmem, smem, hbm = (pl.BlockSpec(memory_space=m) for m in (pltpu.VMEM, pltpu.SMEM, pl.ANY))
    dma = pltpu.SemaphoreType.DMA
    v = pltpu.VMEM
    cw = width_d // CHUNKS
    scratch = [
        v((CHUNKS, 16, lanes, cw), BF16),
        v((16, share, width_d), BF16),
        v((width_h, width_d), BF16),
        v((CHUNKS, width_h, cw), BF16),
        v((lanes, width_d), BF16),
        v((tops, micros, toks, width_h), BF16),
        v((16 * micros * CAP, tops * lanes), BF16),
        v((16, micros * CAP, width_h), BF16),
        v((16, micros * CAP, width_h), BF16),
        v((16, lanes, width_h), BF16),
        v((16, lanes, width_h), F32),
        v((16, 8, lanes), F32),
        v((16, 8, lanes), F32),
        v((16, micros * CAP, width_h), BF16),
        v((16, micros * CAP, width_h), BF16),
        v((CHUNKS, cw, width_h), BF16),
        v((CHUNKS, 32, width_h), BF16),
        v((CHUNKS, 32, width_h), BF16),
        v((CHUNKS, 3, 64, width_h), BF16),
        v((CHUNKS, 3, 64, width_h), BF16),
        v((CHUNKS, 32, width_h), BF16),
        v((CHUNKS, 32, width_h), BF16),
        v((CHUNKS, 32, width_h), F32),
        v((share, width_d), BF16),
        v((tops, lanes, width_h), BF16),
        dma((22,)),
        dma((CHUNKS + 1, PIECES)),
        dma((CHUNKS + 1, PIECES)),
        dma((16,)), dma((16,)),
        dma((16,)), dma((16,)),
        dma((16,)), dma((16,)),
        dma((2, 4, 2)), dma((2, 4, 2)),
        dma((1,)), dma((1,)),
        dma((CHUNKS, 4, 2)), dma((CHUNKS, 4, 2)),
        dma((CHUNKS,)), dma((CHUNKS,)),
    ]
    slot_grads, new_weights, grads = pl.pallas_call(
        kernel,
        out_shape=(
            jax.ShapeDtypeStruct(hid_t.shape, BF16),
            jax.ShapeDtypeStruct((width_h, width_d), BF16),
            jax.ShapeDtypeStruct((out_rows, width_h), BF16),
        ),
        in_specs=[vmem, vmem, smem, smem, hbm, hbm, hbm],
        out_specs=(hbm, hbm, vmem),
        scratch_shapes=scratch,
        compiler_params=pltpu.CompilerParams(
            collective_id=0, has_side_effects=True, vmem_limit_bytes=60 * 1024 * 1024
        ),
    )(ids_t, gates_t, old_place, new_place, hid_t, cot, old_weights[0])
    return slot_grads.transpose(0, 2, 1, 3), new_weights[None], grads.T[None]


def solution(mesh):
    in_specs = (
        P(None, ("grp", "ep"), None),
        P(None, ("grp", "ep"), None),
        P(None, ("grp", "ep"), None, None),
        P(None, ("grp", "ep"), None),
        P(),
        P(),
        P("ep", None, None),
    )
    out_specs = (P(None, ("grp", "ep"), None, None), P("ep", None, None), P("ep", None, "grp"))
    return jax.shard_map(local, mesh=mesh, in_specs=in_specs, out_specs=out_specs, check_vma=False)
```

time: 398 us -> 180 us (0.45)
  waiting for transfers between devices: 290 us -> 0 us
  Pallas kernels: 0 us -> 168 us
  matrix products: 30.5 us -> 0 us
  blocking collectives: 22.1 us -> 0 us
  between operations: 16 us -> 0.64 us
  local copies, waits for them, and re-layouts: 23.4 us -> 10.1 us
  starting transfers between devices: 11.3 us -> 0 us
  other arithmetic: 4.24 us -> 0 us
    pallas_call x0 -> x1, Pallas kernels: none -> 168 us  [local(): pl.pallas_call(kernel, out_shape=(jax.ShapeDtypeStruct(hid_t.shape, BF16)...]
    all_gather x3 -> x0, waiting for transfers between devices: 140 us -> none  [the longest x1 85.5 us: local(): cot_all = lax.all_gather(cotangent, 'ep')]
    unnamed x5 -> x0, waiting for transfers between devices: 90.7 us -> none
    all_to_all x2 -> x0, waiting for transfers between devices: 59.1 us -> none  [the longest x1 30.3 us: local(): lax.all_to_all(back, 'ep', split_axis=0, concat_axis=0, tiled=True)]
    dot_general x8 -> x0, matrix products: 30.5 us -> none  [the longest x1 14.3 us: local(): lax.dot_general(cot_rows, hid_rows.reshape(-1, width_h), (((0,), (0,)), (...]
    all_gather x1 -> x0, blocking collectives: 22.1 us -> none  [local(): meta_all = lax.all_gather(meta, 'ep')]
    all_to_all x2 -> x0, starting transfers between devices: 10.9 us -> none  [the longest x1 5.48 us: local(): lax.all_to_all(hid_out, 'ep', split_axis=0, concat_axis=0, tiled=True)]
    unnamed x19 -> x5, local copies, waits for them, and re-layouts: 15.9 us -> 7.39 us
  transfers between devices with their start and end apart: 6 -> 0, of which waited for: 6 -> 0; matrix products, arithmetic and copies ran while one was open for 14% -> 0% of each run, Pallas kernels for 0% -> 0%
where the time goes in v2:
time: 180 us; the launch traced here: 179 us
  Pallas kernels  168 us (93%)
  local copies, waits for them, and re-layouts  10.1 us (6%)
    pallas_call x1, Pallas kernels, local(): pl.pallas_call(kernel, out_shape=(jax.ShapeDtypeStruct(hid_t.shape, BF16)...  168 us
    unnamed x5, local copies, waits for them, and re-layouts  7.39 us

profile of v2, /device:TPU:2, one launch (start us, length us, event | category | flops | bytes accessed | tf_op | source)
XLA Modules:
  0.0 178.7 jit_solution(11796723107547788123)
XLA Ops:
  0.6 1.4 reshape.15.ids
  2.0 1.4 reshape.16.gates
  3.4 167.9 %shard_map.94 = (bf16[2,6,64,768]{3,2,1,0:T(8,128)(2,1)}, bf16[768,2560]{1,0:T(8,128)(2,1)}, bf16[160,768]{1,0:T(8,128)(2,1)}) custom-call(s32[6,128]{1,0:T(8,128)} %reshape.15.ids, f32[6,128]{1,0:T(8,128)} %reshape.16.gates, s32[16]{0:T(128)} %old_place.1, s32[16]{0:T(128)} %new_place.1, bf16[2,6,64,768]{3,2,1,0:T(8,128)(2,1)} %bitcast.13, ...), custom_call_target="tpu_custom_call" | custom-call | tf_op jit(solution)/shard_map/pallas_call | solution.py:492
  171.3 2.4 %copy.13 = bf16[2,64,6,768]{3,1,2,0:T(8,128)(2,1)} copy(bf16[2,64,6,768]{3,1,2,0:T(8,128)(2,1)} %bitcast.12) | data formatting | bytes 2359296
  173.7 0.0 copy-start
  173.7 4.3 %copy.14 = bf16[1,768,2560]{2,1,0:T(8,128)(2,1)} copy(bf16[1,768,2560]{2,1,0:T(8,128)(2,1)} %bitcast.11) | data formatting | bytes 7864320
  178.0 0.0 copy-done
  178.0 0.7 copy.15
Async XLA Ops:
  173.7 4.3 %copy-start = (bf16[160,768]{1,0:T(8,128)(2,1)S(1)}, bf16[160,768]{1,0:T(8,128)(2,1)}, u32[]{:S(2)}) copy-start(bf16[160,768]{1,0:T(8,128)(2,1)} %get-tuple-element.8) | copy-start | bytes 737284

commit v3 on v2

v3 whole, which is shorter than its diff:
```python
import functools

import jax
import jax.numpy as jnp
from jax import lax
from jax.experimental import pallas as pl
from jax.experimental.pallas import tpu as pltpu
from jax.sharding import PartitionSpec as P

F32 = jnp.float32
BF16 = jnp.bfloat16
MESH = pl.DeviceIdType.MESH

CHUNKS = 5
PIECES = 10
CAP = 32
W_PARTS = ((0, 16), (16, 32))


def dot(a, b, ca, cb):
    return lax.dot_general(a, b, (((ca,), (cb,)), ((), ())), preferred_element_type=F32)


def kernel(
    ids, gates, old_place, new_place, hid, cot, w_old, ret_out, row_out, w_out, eg_out,
    gat, wsh_0, wsh_1, w_res, w_perm, cot_v, hid_v, a_mat, hid_send, hid_in, hid_rows, acc,
    meta_send, meta_in, ret_send, ret_in, part, rs_r0, rs_l0, rs_r, rs_l, ysend, yrecv, eg_sum,
    w_own, relay_y, relay_x,
    loc, ag_s, ag_r, hid_s, hid_r, meta_s, meta_r, ret_s, ret_r, z_s, z_r, zy_s, zy_r, c_s, c_r, cy_s, cy_r,
):
    g = lax.axis_index("grp")
    me = lax.axis_index("ep")
    z, yl = g // 2, g % 2
    core, xx, yh = me % 2, (me // 2) % 4, me // 8
    share = w_own.shape[0]
    ep_n = 16
    width_h = hid_v.shape[-1]

    def at_ep(dy=0, dx=0, dc=0):
        return (((yh + dy) % 2) * 4 + (xx + dx + 4) % 4) * 2 + (core + dc) % 2

    def to_ep(e):
        return (g, e)

    zp, zm = (((z + 1) % 8) * 2 + yl, me), (((z + 7) % 8) * 2 + yl, me)
    yp = (z * 2 + 1 - yl, me)
    left, right, yside, other = at_ep(dx=-1), at_ep(dx=1), at_ep(dy=1), at_ep(dc=1)

    def rdma(src, dst, ss, rs, dev):
        return pltpu.make_async_remote_copy(
            src_ref=src, dst_ref=dst, send_sem=ss, recv_sem=rs, device_id=dev, device_id_type=MESH
        )

    barrier = pltpu.get_barrier_semaphore()
    for d in range(1, ep_n):
        pl.semaphore_signal(barrier, 1, device_id=to_ep((me + d) % ep_n), device_id_type=MESH)
    for dev in (zp, zm, yp):
        pl.semaphore_signal(barrier, 1, device_id=dev, device_id_type=MESH)

    loads = [pltpu.make_async_copy(cot, cot_v, loc.at[0]), pltpu.make_async_copy(w_old, w_res, loc.at[1])]
    loads += [pltpu.make_async_copy(hid.at[:, k], hid_v.at[k], loc.at[2 + k]) for k in range(6)]

    def my_rows(w):
        lo, n = W_PARTS[w]
        return w_old.at[pl.ds(pl.multiple_of(g * share + lo, 16), n)]

    def by_core(e):
        return (e % 2) * 8 + e // 2

    def w_part(src, w):
        return (wsh_0, wsh_1)[w].at[src]

    mine = by_core(me)

    loads += [pltpu.make_async_copy(my_rows(w), w_part(mine, w), loc.at[8 + w]) for w in (0, 1)]
    for cp in loads:
        cp.start()
    pl.semaphore_wait(barrier, ep_n - 1 + 3)

    def block(job, src):
        if isinstance(job, str):
            return w_part(src, int(job))
        return gat.at[job, src]

    def half(job, src, h):
        if isinstance(job, str):
            cols = wsh_0.shape[2] // 2
            return (wsh_0, wsh_1)[int(job)].at[src, :, pl.ds(h * cols, cols)]
        return gat.at[job, src, pl.ds(h * 64, 64)]

    def number(job):
        if isinstance(job, str):
            return int(job)
        return job + 2

    def ag_send(job, piece, ref, dev, src=None):
        j = number(job)
        rdma(ref if src is None else src, ref, ag_s.at[j], ag_r.at[j, piece], to_ep(dev)).start()

    def ag_wait(job, piece, ref):
        j = number(job)
        rdma(ref, ref, ag_s.at[j], ag_r.at[j, piece], to_ep(other)).wait_recv()

    b_left, b_right, b_side = by_core(left), by_core(right), by_core(yside)
    b_x2 = by_core(at_ep(dx=2))
    b_yleft, b_yright, b_yx2 = by_core(at_ep(dy=1, dx=-1)), by_core(at_ep(dy=1, dx=1)), by_core(at_ep(dy=1, dx=2))
    plane, far_plane = core * 8 + yh * 4, core * 8 + (1 - yh) * 4
    o_plane, o_far_plane = (1 - core) * 8 + yh * 4, (1 - core) * 8 + (1 - yh) * 4

    def ag0(job):
        own = block(job, mine)
        src = my_rows(int(job)) if isinstance(job, str) else None
        ag_send(job, 0, own, right, src)
        ag_send(job, 1, own, left, src)
        ag_send(job, 2, own, yside, src)

    def ag1(job):
        ag_wait(job, 0, block(job, b_left))
        ag_send(job, 3, half(job, b_left, 0), right)
        ag_wait(job, 1, block(job, b_right))
        ag_send(job, 4, half(job, b_right, 1), left)
        ag_wait(job, 2, block(job, b_side))
        ag_send(job, 5, block(job, b_side), right)
        ag_send(job, 6, block(job, b_side), left)

    def ag2(job):
        ag_wait(job, 3, half(job, b_x2, 0))
        ag_wait(job, 4, half(job, b_x2, 1))
        ag_send(job, 7, block(job, b_x2), yside)
        if isinstance(job, str):
            loads[8 + int(job)].wait()
        ag_send(job, 8, block(job, pl.ds(plane, 4)), other)

    def ag3(job):
        ag_wait(job, 5, block(job, b_yleft))
        ag_wait(job, 6, block(job, b_yright))
        ag_wait(job, 7, block(job, b_yx2))
        ag_send(job, 9, block(job, pl.ds(far_plane, 4)), other)

    def ag4(job):
        ag_wait(job, 8, block(job, pl.ds(o_plane, 4)))
        ag_wait(job, 9, block(job, pl.ds(o_far_plane, 4)))

    def ag_drain(job):
        ref = block(job, pl.ds(0, 15))
        rdma(ref, ref, ag_s.at[number(job)], ag_r.at[number(job), 0], to_ep(other)).wait_send()

    ag0("0")
    ag0("1")

    def chooser(c):
        i = lax.broadcasted_iota(jnp.int32, (640, 128), 0)
        j = lax.broadcasted_iota(jnp.int32, (640, 128), 1)
        return (i == (j // 32) * 160 + c * 32 + j % 32).astype(BF16)

    loads[0].wait()

    def perm_cot(c, _):
        sel = chooser(c)
        for q in range(4):
            gat[c, mine, :, q * 128 : (q + 1) * 128] = dot(
                cot_v[:, q * 640 : (q + 1) * 640], sel, 1, 0
            ).astype(BF16)
        return 0

    lax.fori_loop(0, CHUNKS, perm_cot, 0)

    ag1("0")

    lane = lax.broadcasted_iota(jnp.int32, (16, 128), 1)
    row16 = lax.broadcasted_iota(jnp.int32, (16, 128), 0)
    micro = (lane[:1] >= 64).astype(F32)
    ui = lax.broadcasted_iota(jnp.int32, (128, 128), 0)
    uj = lax.broadcasted_iota(jnp.int32, (128, 128), 1)
    upper = ((ui < uj) & ((ui >= 64) == (uj >= 64))).astype(BF16)

    def lanes_of(ref, k):
        both = ref[k]
        return jnp.concatenate([both[0:1], both[1:2]], axis=1)

    slot_of = [jnp.zeros((16, 128), F32), jnp.zeros((16, 128), F32)]
    source = jnp.int32(0)
    for e in range(16):
        slot_of[0] = jnp.where(row16 == e, old_place[e].astype(F32), slot_of[0])
        slot_of[1] = jnp.where(row16 == e, new_place[e].astype(F32), slot_of[1])
        source = source + jnp.where(new_place[e] == me, old_place[e], 0)
    target = [[], []]
    for which in (0, 1):
        slots, hits = [], []
        for k in range(6):
            eq = lanes_of(ids, k) == row16
            slot = jnp.sum(jnp.where(eq, slot_of[which], 0.0), axis=0, keepdims=True)
            slots.append(slot)
            hits.append(row16.astype(F32) == slot)
        routed = sum(h.astype(F32) for h in hits)
        rank = dot(routed.astype(BF16), upper, 1, 0)
        for k in range(6):
            nth = jnp.sum(jnp.where(hits[k], rank, 0.0), axis=0, keepdims=True)
            target[which].append(slots[k] * (2 * CAP) + micro * CAP + nth)
        coded = jnp.where(routed > 0.5, rank + micro * CAP, -1.0)
        for s in range(16):
            meta_send[s, which : which + 1, :] = coded[s : s + 1, :]

    for k in range(6):
        row_out[k : k + 1, :] = target[0][k]

    def build(which):
        rows = lax.broadcasted_iota(jnp.int32, (1024, 128), 0).astype(F32)
        for k in range(6):
            a_mat[:, k * 128 : (k + 1) * 128] = jnp.where(
                rows == target[which][k], lanes_of(gates, k), 0.0
            ).astype(BF16)

    def spread_out(src, dst, ss, rs, ways=range(1, 16)):
        for d in ways:
            e = (me + d) % ep_n
            rdma(src.at[e], dst.at[me], ss.at[0], rs.at[0], to_ep(e)).start()

    def spread_wait(dst, ss, rs):
        ref = dst.at[pl.ds(0, ep_n - 1)]
        rdma(ref, ref, ss.at[0], rs.at[0], to_ep(other)).wait_recv()

    def spread_drain(src, ss, rs):
        ref = src.at[pl.ds(0, ep_n - 1)]
        rdma(ref, ref, ss.at[0], rs.at[0], to_ep(other)).wait_send()

    here, near, far = me % 8, yh * 8, (1 - yh) * 8
    side = far + here
    upper_rows, lower_rows = pl.ds(0, CAP), pl.ds(CAP, CAP)

    def swap(which, src, dst, piece, dev):
        ss, rs = (hid_s, hid_r) if which == 0 else (ret_s, ret_r)
        return rdma(src, dst, ss.at[0], rs.at[piece], to_ep(dev))

    def swap_far(which, send):
        ya, xb = relay_y.at[which], relay_x.at[which]
        for d in range(1, 8):
            t = (here + d) % 8
            swap(which, send.at[far + t, lower_rows], xb.at[here], 0, near + t).start()
        swap(which, send.at[pl.ds(far, 8), upper_rows], ya, 1, side).start()
        relay_x[which, here] = send[side, lower_rows]

    def swap_near(which, send, into):
        for d in range(1, 8):
            t = (here + d) % 8
            swap(which, send.at[near + t], into.at[me], 2, near + t).start()
        into[me] = send[me]

    def swap_pass(which, into):
        ya, xb = relay_y.at[which], relay_x.at[which]
        swap(which, xb.at[pl.ds(0, 7)], xb.at[pl.ds(0, 7)], 0, side).wait_recv()
        swap(which, xb, into.at[pl.ds(near, 8), lower_rows], 3, side).start()
        swap(which, ya, ya, 1, side).wait_recv()
        for d in range(1, 8):
            t = (here + d) % 8
            swap(which, ya.at[t], into.at[side, upper_rows], 4, near + t).start()
        into[side, upper_rows] = relay_y[which, here]

    def swap_wait(which, into):
        seven = pl.ds(0, 7)
        swap(which, into.at[seven], into.at[seven], 2, side).wait_recv()
        ref = into.at[pl.ds(far, 8), lower_rows]
        swap(which, ref, ref, 3, side).wait_recv()
        ref = into.at[seven, upper_rows]
        swap(which, ref, ref, 4, side).wait_recv()

    def swap_drain(which):
        ref = hid_rows.at[pl.ds(0, 11)]
        swap(which, ref, ref, 0, side).wait_send()

    spread_out(meta_send, meta_in, meta_s, meta_r)
    meta_in[me] = meta_send[me]
    ag1("1")
    ag2("0")
    ag0(0)
    build(1)
    for cp in loads[2:8]:
        cp.wait()
    def pack(i, _):
        rows = pl.ds(pl.multiple_of(i * 256, 256), 256)
        res = dot(a_mat[rows, :], hid_v[...].reshape(6 * 128, width_h), 1, 0).astype(BF16)
        hid_send[pl.ds(i * 4, 4)] = res.reshape(4, 64, width_h)
        return 0

    lax.fori_loop(0, 4, pack, 0)

    ag3("0")
    ag2("1")


    def w_rows(w, zz, yy):
        lo, n = W_PARTS[w]
        return w_out.at[(zz + 16) % 8, yy, pl.ds(lo, n)]

    def w_pair(w, zz):
        lo, n = W_PARTS[w]
        return w_out.at[(zz + 16) % 8, :, pl.ds(lo, n)]

    def own_part(w):
        lo, n = W_PARTS[w]
        return w_own.at[pl.ds(lo, n)]

    def z_copy(w, src, dst, way, step, yy):
        return rdma(src, dst, z_s.at[w], z_r.at[w, way, step, yy], zp if way == 0 else zm)

    def keep_own(w):
        return pltpu.make_async_copy(own_part(w), w_rows(w, z, yl), loc.at[10 + w])

    def z_begin(w):
        lo, n = W_PARTS[w]
        ag4(str(w))
        w_own[lo : lo + n] = (wsh_0, wsh_1)[w][by_core(source)]
        rdma(own_part(w), w_rows(w, z, yl), zy_s.at[w], zy_r.at[w], yp).start()
        for way in (0, 1):
            z_copy(w, own_part(w), w_rows(w, z, yl), way, 0, yl).start()
        keep_own(w).start()

    def zag(w, step):
        if step == 0:
            ref = w_rows(w, z, 1 - yl)
            rdma(ref, ref, zy_s.at[w], zy_r.at[w], yp).wait_recv()
            for way in (0, 1):
                z_copy(w, ref, ref, way, 0, 1 - yl).start()
            return
        for way in (0, 1):
            zz = z - step if way == 0 else z + step
            if step == 1:
                for yy in (0, 1):
                    ref = w_rows(w, zz, yy)
                    z_copy(w, ref, ref, way, 0, yy).wait_recv()
            else:
                ref = w_pair(w, zz) if step < 4 else w_rows(w, zz, way)
                z_copy(w, ref, ref, way, step - 1, 0).wait_recv()
            if step < 4:
                ref = w_pair(w, zz) if step < 3 else w_rows(w, zz, way)
                z_copy(w, ref, ref, way, step, 0).start()

    z_begin(0)
    ag1(0)
    ag0(1)
    swap_far(0, hid_send)
    zag(0, 0)
    loads[1].wait()

    def perm_w(c, _):
        sel = chooser(c)
        for q in range(4):
            w_perm[c, :, q * 128 : (q + 1) * 128] = dot(
                w_res[:, q * 640 : (q + 1) * 640], sel, 1, 0
            ).astype(BF16)
        return 0

    ag3("1")
    lax.fori_loop(0, 2, perm_w, 0)
    ag2(0)
    z_begin(1)
    ag1(1)
    swap_near(0, hid_send, hid_in)
    lax.fori_loop(2, CHUNKS, perm_w, 0)
    ag3(0)
    zag(0, 1)
    zag(1, 0)
    acc[...] = jnp.zeros_like(acc)
    ag2(1)
    swap_pass(0, hid_in)
    ag0(2)

    def c_rows(c, zz, h=None):
        start = pl.multiple_of(((zz + 16) % 8) * 64 + (0 if h is None else h * 32), 32)
        return part.at[c, pl.ds(start, 64 if h is None else 32)]

    def add_into(ref, other_ref):
        ref[...] = (ref[...].astype(F32) + other_ref[...].astype(F32)).astype(BF16)

    def rs_move(c, step, way, src, dst):
        return rdma(src, dst, c_s.at[c], c_r.at[c, step, way], zp if way == 0 else zm)

    def rs(c, step):
        if step == 0:
            rs_move(c, 0, 0, c_rows(c, z + 4, 0), rs_r0.at[c]).start()
            rs_move(c, 0, 1, c_rows(c, z - 4, 1), rs_l0.at[c]).start()
            return
        if step == 5:
            rdma(yrecv.at[c], yrecv.at[c], cy_s.at[c], cy_r.at[c], yp).wait_recv()
            tot = eg_sum[c] + yrecv[c].astype(F32)
            eg_out[pl.ds(pl.multiple_of(c * 32, 32), 32), :] = (tot / 16.0).astype(BF16)
            return
        if step == 4:
            rs_move(c, 3, 0, rs_r.at[c, 2], rs_r.at[c, 2]).wait_recv()
            rs_move(c, 3, 1, rs_l.at[c, 2], rs_l.at[c, 2]).wait_recv()
            for h in (0, 1):
                rows = pl.ds(h * 32, 32)
                tot = (
                    c_rows(c, z, h)[...].astype(F32)
                    + rs_r[c, 2, rows, :].astype(F32)
                    + rs_l[c, 2, rows, :].astype(F32)
                )

                @pl.when(yl == h)
                def _():
                    eg_sum[c] = tot

                @pl.when(yl != h)
                def _():
                    ysend[c] = tot.astype(BF16)

            rdma(ysend.at[c], yrecv.at[c], cy_s.at[c], cy_r.at[c], yp).start()
            return
        for way, first, later in ((0, rs_r0, rs_r), (1, rs_l0, rs_l)):
            tgt = z + 4 - step if way == 0 else z - 4 + step
            if step == 1:
                rs_move(c, 0, way, first.at[c], first.at[c]).wait_recv()
                add_into(c_rows(c, tgt, way), first.at[c])
            else:
                rs_move(c, step - 1, way, later.at[c, step - 2], later.at[c, step - 2]).wait_recv()
                add_into(c_rows(c, tgt), later.at[c, step - 2])
            rs_move(c, step, way, c_rows(c, tgt), later.at[c, step - 1]).start()

    def rs_drain(c):
        ref = part.at[c, pl.ds(0, 2 * (32 + 3 * 64))]
        rdma(ref, ref, c_s.at[c], c_r.at[c, 0, 0], zp).wait_send()
        rdma(ysend.at[c], ysend.at[c], cy_s.at[c], cy_r.at[c], yp).wait_send()

    code_row = lax.broadcasted_iota(jnp.int32, (64, 128), 0).astype(F32)

    def place_rows(s, _):
        sel = (code_row == meta_in[s, 1:2, :]).astype(BF16)
        hid_rows[by_core(s)] = dot(sel, hid_in[s], 0, 0).astype(BF16)
        return 0


    def back(c):
        def body(i, _):
            rows = pl.ds(i * 4, 4)
            res = dot(gat[c, rows].reshape(512, 512), w_perm[c], 1, 1)
            acc[rows] += res.reshape(4, 128, width_h)
            return 0

        lax.fori_loop(0, 4, body, 0)

    def pack_back(first):
        def body(t, _):
            e = first + t
            sel = (code_row == meta_in[e, 0:1, :]).astype(BF16)
            ret_send[e] = dot(sel, acc[by_core(e)].astype(BF16), 1, 0).astype(BF16)
            return 0

        lax.fori_loop(0, 8, body, 0)

    def weight_part(c):
        def body(n, _):
            rows = pl.ds(pl.multiple_of(n * 256, 256), 256)
            left_rows = gat[c, :, :, rows].reshape(ep_n * 128, 256)
            part[c, rows] = dot(left_rows, hid_rows[...].reshape(ep_n * 128, width_h), 0, 0).astype(BF16)
            return 0

        lax.fori_loop(0, 2, body, 0)

    def inside(c, f):
        pl.when((c >= 0) & (c < CHUNKS))(lambda: f(c))

    def sums(i):
        for step in (5, 4, 3, 2, 1):
            inside(i - step, lambda c: rs(c, step))

    ag4(0)
    back(0)
    zag(0, 2)
    ag3(1)
    ag1(2)
    zag(1, 1)
    ag4(1)
    back(1)
    zag(0, 3)
    ag0(3)
    ag2(2)
    spread_wait(meta_in, meta_s, meta_r)
    swap_wait(0, hid_in)
    lax.fori_loop(0, ep_n, place_rows, 0)
    weight_part(0)
    rs(0, 0)
    ag3(2)
    ag1(3)
    ag0(4)
    zag(1, 2)
    weight_part(1)
    rs(1, 0)
    rs(0, 1)

    def tick(i, _):
        inside(i + 1, ag2)
        inside(i + 2, ag1)
        ag4(i)
        back(i)
        sums(i)
        weight_part(i)
        rs(i, 0)
        inside(i + 1, ag3)
        pl.when(i == 2)(lambda: zag(1, 3))
        return 0

    lax.fori_loop(2, CHUNKS, tick, 0)
    pack_back(far)
    swap_far(1, ret_send)
    pack_back(near)
    swap_near(1, ret_send, ret_in)

    def tail(i, _):
        sums(i)
        return 0

    lax.fori_loop(CHUNKS, CHUNKS + 2, tail, 0)
    swap_pass(1, ret_in)
    lax.fori_loop(CHUNKS + 2, CHUNKS + 5, tail, 0)
    swap_wait(1, ret_in)
    keep_ret = pltpu.make_async_copy(ret_in, ret_out, loc.at[12])
    keep_ret.start()
    zag(0, 4)
    zag(1, 4)

    ag_drain("0")
    ag_drain("1")

    def drain(c, _):
        ag_drain(c)
        rs_drain(c)
        return 0

    lax.fori_loop(0, CHUNKS, drain, 0)
    spread_drain(meta_send, meta_s, meta_r)
    swap_drain(0)
    swap_drain(1)
    for w in (0, 1):
        keep_own(w).wait()
        rdma(own_part(w), own_part(w), zy_s.at[w], zy_r.at[w], yp).wait_send()
        lo, n = W_PARTS[w]
        sent = w_out.at[pl.ds(0, 7), :, pl.ds(lo, n)]
        z_copy(w, sent, sent, 0, 0, 0).wait_send()
    keep_ret.wait()


def finish(ret_h, rows_at, gates, w_in, eg_in, sg_out, w_out, eg_out, ret, w_v, sems):
    load = pltpu.make_async_copy(ret_h, ret, sems.at[sems.shape[0] - 1])
    load.start()
    pieces = (sems.shape[0] - 1) // 2
    n = w_in.shape[0] // pieces
    rows_of = [pl.ds(p * n, n) for p in range(pieces)]
    ups = [pltpu.make_async_copy(w_in.at[r], w_v.at[r], sems.at[p]) for p, r in enumerate(rows_of)]
    downs = [pltpu.make_async_copy(w_v.at[r], w_out.at[r], sems.at[pieces + p]) for p, r in enumerate(rows_of)]
    for cp in ups:
        cp.start()
    eg_out[...] = eg_in[...]
    load.wait()
    rows = lax.broadcasted_iota(jnp.int32, (1024, 128), 0).astype(F32)
    for k in range(6):
        for p in range(k * pieces // 6, (k + 1) * pieces // 6):
            ups[p].wait()
            downs[p].start()
        both = gates[k]
        gate = jnp.concatenate([both[0:1], both[1:2]], axis=1)
        sel = jnp.where(rows == rows_at[k : k + 1, :], gate, 0.0).astype(BF16)
        got = dot(sel, ret[...].reshape(1024, ret.shape[-1]), 0, 0).astype(BF16)
        sg_out[0, k] = got[:64]
        sg_out[1, k] = got[64:]
    for cp in downs:
        cp.wait()


def local(expert_ids, gates, hidden, cotangent, old_place, new_place, old_weights):
    micros, toks, tops = expert_ids.shape
    width_h, width_d = old_weights.shape[1:]
    lanes = micros * toks
    share = width_h // 16
    out_rows = width_d // 16
    ids_t = expert_ids.transpose(2, 0, 1)
    gates_t = gates.transpose(2, 0, 1)
    hid_t = hidden.transpose(0, 2, 1, 3)
    cot = cotangent.reshape(lanes, width_d)
    vmem, smem, hbm = (pl.BlockSpec(memory_space=m) for m in (pltpu.VMEM, pltpu.SMEM, pl.ANY))
    dma = pltpu.SemaphoreType.DMA
    v = pltpu.VMEM
    cw = width_d // CHUNKS
    scratch = [
        v((CHUNKS, 16, lanes, cw), BF16),
        v((16, W_PARTS[0][1], width_d), BF16),
        v((16, W_PARTS[1][1], width_d), BF16),
        v((width_h, width_d), BF16),
        v((CHUNKS, width_h, cw), BF16),
        v((lanes, width_d), BF16),
        v((tops, micros, toks, width_h), BF16),
        v((16 * micros * CAP, tops * lanes), BF16),
        v((16, micros * CAP, width_h), BF16),
        v((16, micros * CAP, width_h), BF16),
        v((16, lanes, width_h), BF16),
        v((16, lanes, width_h), F32),
        v((16, 8, lanes), F32),
        v((16, 8, lanes), F32),
        v((16, micros * CAP, width_h), BF16),
        v((16, micros * CAP, width_h), BF16),
        v((CHUNKS, cw, width_h), BF16),
        v((CHUNKS, 32, width_h), BF16),
        v((CHUNKS, 32, width_h), BF16),
        v((CHUNKS, 3, 64, width_h), BF16),
        v((CHUNKS, 3, 64, width_h), BF16),
        v((CHUNKS, 32, width_h), BF16),
        v((CHUNKS, 32, width_h), BF16),
        v((CHUNKS, 32, width_h), F32),
        v((share, width_d), BF16),
        v((2, 8, CAP, width_h), BF16),
        v((2, 8, CAP, width_h), BF16),
        dma((13,)),
        dma((CHUNKS + 2,)),
        dma((CHUNKS + 2, PIECES)),
        dma((1,)), dma((5,)),
        dma((1,)), dma((1,)),
        dma((1,)), dma((5,)),
        dma((2,)), dma((2, 2, 4, 2)),
        dma((2,)), dma((2,)),
        dma((CHUNKS,)), dma((CHUNKS, 4, 2)),
        dma((CHUNKS,)), dma((CHUNKS,)),
    ]
    ret, rows_at, weights, grads = pl.pallas_call(
        kernel,
        out_shape=(
            jax.ShapeDtypeStruct((16, micros * CAP, width_h), BF16),
            jax.ShapeDtypeStruct((8, lanes), F32),
            jax.ShapeDtypeStruct((8, 2, share, width_d), BF16),
            jax.ShapeDtypeStruct((out_rows, width_h), BF16),
        ),
        in_specs=[vmem, vmem, smem, smem, hbm, hbm, hbm],
        out_specs=(hbm, vmem, hbm, vmem),
        scratch_shapes=scratch,
        compiler_params=pltpu.CompilerParams(
            collective_id=0, has_side_effects=True, vmem_limit_bytes=60 * 1024 * 1024
        ),
    )(ids_t, gates_t, old_place, new_place, hid_t, cot, old_weights[0])
    weights = weights.reshape(width_h, width_d)
    slot_grads, new_weights, grads = pl.pallas_call(
        finish,
        out_shape=(
            jax.ShapeDtypeStruct(hid_t.shape, BF16),
            jax.ShapeDtypeStruct(weights.shape, BF16),
            jax.ShapeDtypeStruct(grads.shape, BF16),
        ),
        in_specs=[hbm, vmem, vmem, hbm, vmem],
        out_specs=(vmem, hbm, vmem),
        scratch_shapes=[v(ret.shape, BF16), v(weights.shape, BF16), dma((25,))],
        compiler_params=pltpu.CompilerParams(vmem_limit_bytes=60 * 1024 * 1024),
    )(ret, rows_at, gates_t, weights, grads)
    return slot_grads.transpose(0, 2, 1, 3), new_weights[None], grads.T[None]


def solution(mesh):
    in_specs = (
        P(None, ("grp", "ep"), None),
        P(None, ("grp", "ep"), None),
        P(None, ("grp", "ep"), None, None),
        P(None, ("grp", "ep"), None),
        P(),
        P(),
        P("ep", None, None),
    )
    out_specs = (P(None, ("grp", "ep"), None, None), P("ep", None, None), P("ep", None, "grp"))
    return jax.shard_map(local, mesh=mesh, in_specs=in_specs, out_specs=out_specs, check_vma=False)
```

time: 180 us -> 144 us (0.80)
  Pallas kernels: 168 us -> 142 us
  local copies, waits for them, and re-layouts: 10.1 us -> 0 us
    pallas_call x1 -> x2, Pallas kernels: 168 us -> 142 us  [the longest x1 135 us: local(): pl.pallas_call(kernel, out_shape=(jax.ShapeDtypeStruct((16, micros * CAP,...]
    unnamed x5 -> x0, local copies, waits for them, and re-layouts: 7.39 us -> none
    reshape x2 -> x0, local copies, waits for them, and re-layouts: 2.72 us -> none  [the longest x1 1.36 us: local(): ids_t = expert_ids.transpose(2, 0, 1).reshape(tops, lanes)]
where the time goes in v3:
time: 144 us; the launch traced here: 143 us
  Pallas kernels  142 us (99%)
    pallas_call x1, Pallas kernels, local(): pl.pallas_call(kernel, out_shape=(jax.ShapeDtypeStruct((16, micros * CAP,...  135 us
    pallas_call x1, Pallas kernels, local(): pl.pallas_call(finish, out_shape=(jax.ShapeDtypeStruct(hid_t.shape, BF16)...  7.4 us

profile of v3, /device:TPU:2, one launch (start us, length us, event | category | flops | bytes accessed | tf_op | source)
XLA Modules:
  0.0 143.1 jit_solution(11023791583115391098)
XLA Ops:
  0.6 135.0 %shard_map.94 = (bf16[16,64,768]{2,1,0:T(8,128)(2,1)}, f32[8,128]{1,0:T(8,128)}, bf16[8,2,48,2560]{3,2,1,0:T(8,128)(2,1)}, bf16[160,768]{1,0:T(8,128)(2,1)}) custom-call(s32[6,2,64]{2,1,0:T(2,128)} %bitcast.17, f32[6,2,64]{2,1,0:T(2,128)} %bitcast.15, s32[16]{0:T(128)} %old_place.1, s32[16]{0:T(128)} %new_place.1, bf16[2,6,64,768]{3,2,1,0:T(8,128)(2,1)} %bitcast.13, ...), custom_call_target="tpu_custom_call" | custom-call | tf_op jit(solution)/shard_map/pallas_call | solution.py:622
  135.7 7.4 %shard_map.95 = (bf16[2,6,64,768]{3,2,1,0:T(8,128)(2,1)}, bf16[768,2560]{1,0:T(8,128)(2,1)}, bf16[160,768]{1,0:T(8,128)(2,1)}) custom-call(bf16[16,64,768]{2,1,0:T(8,128)(2,1)} %get-tuple-element.10.ret_h, f32[8,128]{1,0:T(8,128)} %get-tuple-element.11.rows_at, f32[6,2,64]{2,1,0:T(2,128)} %bitcast.16, bf16[768,2560]{1,0:T(8,128)(2,1)} %bitcast.12, ...), custom_call_target="tpu_custom_call" | custom-call | tf_op jit(solution)/shard_map/pallas_call | solution.py:638

commit v4 on v3

--- a/solution.py
+++ b/solution.py
@@ -166,6 +166,9 @@
     lax.fori_loop(0, CHUNKS, perm_cot, 0)
 
     ag1("0")
+    ag1("1")
+    ag0(0)
+    ag2("0")
 
     lane = lax.broadcasted_iota(jnp.int32, (16, 128), 1)
     row16 = lax.broadcasted_iota(jnp.int32, (16, 128), 0)
@@ -270,9 +273,6 @@
 
     spread_out(meta_send, meta_in, meta_s, meta_r)
     meta_in[me] = meta_send[me]
-    ag1("1")
-    ag2("0")
-    ag0(0)
     build(1)
     for cp in loads[2:8]:
         cp.wait()
@@ -423,29 +423,26 @@
 
     code_row = lax.broadcasted_iota(jnp.int32, (64, 128), 0).astype(F32)
 
-    def place_rows(s, _):
-        sel = (code_row == meta_in[s, 1:2, :]).astype(BF16)
-        hid_rows[by_core(s)] = dot(sel, hid_in[s], 0, 0).astype(BF16)
-        return 0
+    def place_rows():
+        for s in range(ep_n):
+            sel = (code_row == meta_in[s, 1:2, :]).astype(BF16)
+            hid_rows[by_core(s)] = dot(sel, hid_in[s], 0, 0).astype(BF16)
 
 
     def back(c):
         def body(i, _):
-            rows = pl.ds(i * 4, 4)
-            res = dot(gat[c, rows].reshape(512, 512), w_perm[c], 1, 1)
-            acc[rows] += res.reshape(4, 128, width_h)
+            rows = pl.ds(i * 8, 8)
+            res = dot(gat[c, rows].reshape(1024, 512), w_perm[c], 1, 1)
+            acc[rows] += res.reshape(8, 128, width_h)
             return 0
 
-        lax.fori_loop(0, 4, body, 0)
+        lax.fori_loop(0, 2, body, 0)
 
     def pack_back(first):
-        def body(t, _):
+        for t in range(8):
             e = first + t
             sel = (code_row == meta_in[e, 0:1, :]).astype(BF16)
             ret_send[e] = dot(sel, acc[by_core(e)].astype(BF16), 1, 0).astype(BF16)
-            return 0
-
-        lax.fori_loop(0, 8, body, 0)
 
     def weight_part(c):
         def body(n, _):
@@ -460,7 +457,7 @@
         pl.when((c >= 0) & (c < CHUNKS))(lambda: f(c))
 
     def sums(i):
-        for step in (5, 4, 3, 2, 1):
+        for step in (4, 3, 2, 1):
             inside(i - step, lambda c: rs(c, step))
 
     ag4(0)
@@ -476,7 +473,7 @@
     ag2(2)
     spread_wait(meta_in, meta_s, meta_r)
     swap_wait(0, hid_in)
-    lax.fori_loop(0, ep_n, place_rows, 0)
+    place_rows()
     weight_part(0)
     rs(0, 0)
     ag3(2)
@@ -499,9 +496,16 @@
         pl.when(i == 2)(lambda: zag(1, 3))
         return 0
 
-    lax.fori_loop(2, CHUNKS, tick, 0)
+    lax.fori_loop(2, CHUNKS - 1, tick, 0)
+
+    last = CHUNKS - 1
+    ag4(last)
+    back(last)
+    weight_part(last)
+    rs(last, 0)
     pack_back(far)
     swap_far(1, ret_send)
+    sums(last)
     pack_back(near)
     swap_near(1, ret_send, ret_in)
 
@@ -511,7 +515,9 @@
 
     lax.fori_loop(CHUNKS, CHUNKS + 2, tail, 0)
     swap_pass(1, ret_in)
-    lax.fori_loop(CHUNKS + 2, CHUNKS + 5, tail, 0)
+    lax.fori_loop(CHUNKS + 2, CHUNKS + 4, tail, 0)
+    for c in range(CHUNKS):
+        rs(c, 5)
     swap_wait(1, ret_in)
     keep_ret = pltpu.make_async_copy(ret_in, ret_out, loc.at[12])
     keep_ret.start()
@@ -539,10 +545,10 @@
     keep_ret.wait()
 
 
-def finish(ret_h, rows_at, gates, w_in, eg_in, sg_out, w_out, eg_out, ret, w_v, sems):
-    load = pltpu.make_async_copy(ret_h, ret, sems.at[sems.shape[0] - 1])
+def finish(ret_h, rows_at, gates, w_in, eg_in, sg_out, w_out, eg_out, ret, w_v, sg_v, sems):
+    load = pltpu.make_async_copy(ret_h, ret, sems.at[24])
     load.start()
-    pieces = (sems.shape[0] - 1) // 2
+    pieces = 12
     n = w_in.shape[0] // pieces
     rows_of = [pl.ds(p * n, n) for p in range(pieces)]
     ups = [pltpu.make_async_copy(w_in.at[r], w_v.at[r], sems.at[p]) for p, r in enumerate(rows_of)]
@@ -551,6 +557,7 @@
         cp.start()
     eg_out[...] = eg_in[...]
     load.wait()
+    outs = []
     rows = lax.broadcasted_iota(jnp.int32, (1024, 128), 0).astype(F32)
     for k in range(6):
         for p in range(k * pieces // 6, (k + 1) * pieces // 6):
@@ -560,9 +567,10 @@
         gate = jnp.concatenate([both[0:1], both[1:2]], axis=1)
         sel = jnp.where(rows == rows_at[k : k + 1, :], gate, 0.0).astype(BF16)
         got = dot(sel, ret[...].reshape(1024, ret.shape[-1]), 0, 0).astype(BF16)
-        sg_out[0, k] = got[:64]
-        sg_out[1, k] = got[64:]
-    for cp in downs:
+        sg_v[k] = got.reshape(2, 64, got.shape[-1])
+        outs.append(pltpu.make_async_copy(sg_v.at[k], sg_out.at[:, k], sems.at[25 + k]))
+        outs[-1].start()
+    for cp in downs + outs:
         cp.wait()
 
 
@@ -643,8 +651,13 @@
             jax.ShapeDtypeStruct(grads.shape, BF16),
         ),
         in_specs=[hbm, vmem, vmem, hbm, vmem],
-        out_specs=(vmem, hbm, vmem),
-        scratch_shapes=[v(ret.shape, BF16), v(weights.shape, BF16), dma((25,))],
+        out_specs=(hbm, hbm, vmem),
+        scratch_shapes=[
+            v(ret.shape, BF16),
+            v(weights.shape, BF16),
+            v((tops, micros, toks, width_h), BF16),
+            dma((31,)),
+        ],
         compiler_params=pltpu.CompilerParams(vmem_limit_bytes=60 * 1024 * 1024),
     )(ret, rows_at, gates_t, weights, grads)
     return slot_grads.transpose(0, 2, 1, 3), new_weights[None], grads.T[None]

time: 144 us -> 143 us (level)
  Pallas kernels: 142 us -> 140 us
    pallas_call x1, Pallas kernels: 135 us -> 132 us  [local(): pl.pallas_call(kernel, out_shape=(jax.ShapeDtypeStruct((16, micros * CAP,...]
where the time goes in v4:
time: 143 us; the launch traced here: 141 us
  Pallas kernels  140 us (98%)
    pallas_call x1, Pallas kernels, local(): pl.pallas_call(kernel, out_shape=(jax.ShapeDtypeStruct((16, micros * CAP,...  132 us
    pallas_call x1, Pallas kernels, local(): pl.pallas_call(finish, out_shape=(jax.ShapeDtypeStruct(hid_t.shape, BF16)...  7.45 us

profile of v4, /device:TPU:2, one launch (start us, length us, event | category | flops | bytes accessed | tf_op | source)
XLA Modules:
  0.0 140.7 jit_solution(9027546623811246977)
XLA Ops:
  0.6 132.4 %shard_map.94 = (bf16[16,64,768]{2,1,0:T(8,128)(2,1)}, f32[8,128]{1,0:T(8,128)}, bf16[8,2,48,2560]{3,2,1,0:T(8,128)(2,1)}, bf16[160,768]{1,0:T(8,128)(2,1)}) custom-call(s32[6,2,64]{2,1,0:T(2,128)} %bitcast.17, f32[6,2,64]{2,1,0:T(2,128)} %bitcast.15, s32[16]{0:T(128)} %old_place.1, s32[16]{0:T(128)} %new_place.1, bf16[2,6,64,768]{3,2,1,0:T(8,128)(2,1)} %bitcast.13, ...), custom_call_target="tpu_custom_call" | custom-call | tf_op jit(solution)/shard_map/pallas_call | solution.py:630
  133.1 7.5 %shard_map.95 = (bf16[2,6,64,768]{3,2,1,0:T(8,128)(2,1)}, bf16[768,2560]{1,0:T(8,128)(2,1)}, bf16[160,768]{1,0:T(8,128)(2,1)}) custom-call(bf16[16,64,768]{2,1,0:T(8,128)(2,1)} %get-tuple-element.10.ret_h, f32[8,128]{1,0:T(8,128)} %get-tuple-element.11.rows_at, f32[6,2,64]{2,1,0:T(2,128)} %bitcast.16, bf16[768,2560]{1,0:T(8,128)(2,1)} %bitcast.12, ...), custom_call_target="tpu_custom_call" | custom-call | tf_op jit(solution)/shard_map/pallas_call | solution.py:646
